TPU v7x, 256 devices: a whole 4x4x8 slice. The times are simulated.
256 devices in a mesh: seq: 64 (over x, z, core), head: 4 (over y).
Axes of the slice: x: 4, y: 4, z: 8, core: 2. Of those that a mesh axis runs over, the one named last changes fastest.
Arguments:
- query: bfloat16 [32768, 16, 128], P('seq', 'head'), may hold values from -6 to 6
- key: bfloat16 [32768, 16, 128], P('seq', 'head'), may hold values from -6 to 6
- value: bfloat16 [32768, 16, 128], P('seq', 'head'), may hold values from -0.5 to 0.5
- beta: float32 [16, 32768], P('head', 'seq'), may hold values from 0.1 to 2
- log_decay: float32 [16, 32768], P('head', 'seq')
- out_weight: bfloat16 [2048, 2048], P('head'), may hold values from -0.125 to 0.125
Outputs:
- mixed: bfloat16 [32768, 2048], P(('seq', 'head'))
All inputs are finite; a program needn't handle non-finite values.
Results may differ from a plain program's by a relative error of at most 0.0075.
Values may be sent and summed in bfloat16 or wider, within the bound.
A program may use at most 128 MiB of HBM per device.

v0:
```python
from functools import partial

import jax
import jax.numpy as jnp
from jax import lax
from jax.sharding import PartitionSpec as P

BLOCK = 128


EXACT = lax.Precision.HIGHEST


def prefix_2(value, axis, join, neutral):
    count, mine = (lax.axis_size(axis), lax.axis_index(axis))
    pieces = lax.all_gather(value, axis)
    total = jnp.full_like(value, 0) + jnp.asarray(neutral, value.dtype)

    def step(position, total):
        longer = join(total, pieces[position])
        return jnp.where(position < mine, longer, total)

    return lax.fori_loop(0, count - 1, step, total)


def unit_rows(tensor):
    widened = tensor.astype(jnp.float32)
    return widened * lax.rsqrt(jnp.sum(widened * widened, axis=-1, keepdims=True) + 1e-06)


def contract(pattern, left_side, right_side):
    return jnp.einsum(pattern, left_side, right_side, precision=EXACT)


def blocks_first(tensor, block_count):
    rows_here, head_count, feature_width = tensor.shape
    return tensor.reshape(
        block_count, rows_here // block_count, head_count, feature_width
    ).transpose(0, 2, 1, 3)


def prepare(query, key, value, beta, log_decay):
    rows_here, head_count, key_width = key.shape
    value_width = value.shape[-1]
    block_count = rows_here // BLOCK
    queries = blocks_first(unit_rows(query), block_count)
    keys_block = blocks_first(unit_rows(key), block_count)
    values_block = blocks_first(value.astype(jnp.float32), block_count)
    strengths = beta.reshape(head_count, block_count, BLOCK).transpose(1, 0, 2)
    log_sums = jnp.cumsum(
        log_decay.reshape(head_count, block_count, BLOCK).transpose(1, 0, 2), axis=-1
    )
    log_spans = log_sums[..., :, None] - log_sums[..., None, :]
    row_index = lax.broadcasted_iota(jnp.int32, (BLOCK, BLOCK), 0)
    col_index = lax.broadcasted_iota(jnp.int32, (BLOCK, BLOCK), 1)
    strict = row_index > col_index
    within = row_index >= col_index
    decay_in = jnp.where(within, jnp.exp(jnp.where(within, log_spans, 0.0)), 0.0)
    key_gram = contract("bhtk,bhsk->bhts", keys_block, keys_block)
    identity_block = jnp.eye(BLOCK, dtype=jnp.float32)
    unit_lower = identity_block + strengths[..., :, None] * key_gram * jnp.where(
        strict, decay_in, 0.0
    )
    growth = jnp.exp(log_sums)
    right_sides = jnp.concatenate(
        [strengths[..., None] * values_block, (strengths * growth)[..., None] * keys_block], axis=-1
    )
    solved = lax.linalg.triangular_solve(
        unit_lower, right_sides, left_side=True, lower=True, unit_diagonal=True
    )
    carried_values = solved[..., :value_width]
    key_factor = solved[..., value_width:]
    query_key = contract("bhtk,bhsk->bhts", queries, keys_block) * decay_in
    fading = keys_block * jnp.exp(log_sums[..., -1:] - log_sums)[..., None]
    end_decay = jnp.exp(log_sums[..., -1])
    return (queries, key_factor, carried_values, query_key, growth, fading, end_decay)


def advance(running_state, pieces, emitting):
    queries, key_factor, carried_values, query_key, growth, fading, end_decay = pieces
    fresh_terms = carried_values - contract("hck,hkw->hcw", key_factor, running_state)
    if emitting:
        result = growth[..., None] * contract("hck,hkw->hcw", queries, running_state) + contract(
            "hcs,hsw->hcw", query_key, fresh_terms
        )
    else:
        result = None
    running_state = end_decay[:, None, None] * running_state + contract(
        "hck,hcw->hkw", fading, fresh_terms
    )
    return (running_state, result)


def body(query, key, value, beta, log_decay, out_weight):
    rows_here, head_count, key_width = key.shape
    value_width = value.shape[-1]
    factors = prepare(query, key, value, beta, log_decay)
    queries, key_factor, carried_values, query_key, growth, fading, end_decay = factors
    block_count = queries.shape[0]
    identity_map = jnp.broadcast_to(
        jnp.eye(key_width, dtype=jnp.float32), (head_count, key_width, key_width)
    )
    identity_pair = jnp.concatenate(
        [identity_map, jnp.zeros((head_count, key_width, value_width), jnp.float32)], axis=-1
    )
    widened_values = jnp.concatenate(
        [jnp.zeros((block_count, head_count, BLOCK, key_width), jnp.float32), carried_values],
        axis=-1,
    )
    widened_pieces = (queries, key_factor, widened_values, query_key, growth, fading, end_decay)
    summary, local_rows = lax.scan(partial(advance, emitting=False), identity_pair, widened_pieces)

    def compose(earlier, later):
        applied = contract("hij,hjw->hiw", later[..., :key_width], earlier)
        return jnp.concatenate(
            [applied[..., :key_width], applied[..., key_width:] + later[..., key_width:]], axis=-1
        )

    prefix = prefix_2(summary, "seq", compose, identity_pair)
    entering = prefix[..., key_width:]
    final_state, outputs = lax.scan(partial(advance, emitting=True), entering, factors)
    attended = (
        outputs.transpose(0, 2, 1, 3)
        .reshape(rows_here, head_count * value_width)
        .astype(jnp.bfloat16)
    )
    mixed = lax.psum_scatter(
        jnp.dot(attended, out_weight, preferred_element_type=jnp.float32),
        "head",
        scatter_dimension=0,
        tiled=True,
    )
    return mixed.astype(jnp.bfloat16)


def solution(mesh):
    in_specs = (
        P("seq", "head", None),
        P("seq", "head", None),
        P("seq", "head", None),
        P("head", "seq"),
        P("head", "seq"),
        P("head", None),
    )
    out_specs = P(("seq", "head"), None)
    return jax.shard_map(body, mesh=mesh, in_specs=in_specs, out_specs=out_specs, check_vma=False)
```

profile of v0, /device:TPU:6, one launch (start us, length us, event | category | flops | bytes accessed | tf_op | source)
XLA Modules:
  0.0 549.2 jit_solution(13255166065465633497)
XLA Ops:
  6.6 2.4 reduce_window_sum.11
  9.9 1.4 fusion.34
  11.4 1.4 convert_multiply_fusion.2
  12.9 3.4 fusion.33
  16.3 158.6 %custom-call.3 = f32[4,4,1,128,128]{3,4,2,1,0:T(8,128)} custom-call(f32[4,4,1,128,128]{4,3,2,1,0:T(8,128)} %fusion.33), custom_call_target="InvertDiagBlocksLowerTriangular" | custom-call | tf_op jit(solution)/shard_map/triangular_solve | solution.py:68
  174.9 1.1 copy.26
  176.4 1.5 bitcast_multiply_fusion.1
  177.9 2.0 fusion.25
  180.0 1.2 fusion.49
  182.2 1.6 concatenate.18
  183.7 1.3 copy.29
  185.1 13.7 %while.38 = (s32[]{:T(128)}, f32[4,128,256]{2,1,0:T(8,128)S(1)}, f32[4,4]{1,0:T(4,128)S(1)}, f32[4,4,128,128]{2,3,1,0:T(8,128)}, f32[4,4,128,256]{3,2,1,0:T(8,128)}, /*index=5*/f32[4,4,128,128]{3,2,1,0:T(8,128)}) while((s32[]{:T(128)}, f32[4,128,256]{2,1,0:T(8,128)S(1)}, f32[4,4]{1,0:T(4,128)S(1)}, f32[4,4,128,128]{2,3,1,0:T(8,128)}, ...), condition=%wide.region_3.4_spmd.clone, body=%wide.region_2.0_spmd.sunk.clone | while | flops 403046400 | bytes 3671673 | solution.py:111
  185.1 1.7 convolution_subtract_fusion.6
  186.9 1.7 convolution_add_fusion.7
  188.6 1.7 convolution_subtract_fusion.6
  190.3 1.7 convolution_add_fusion.7
  192.0 1.7 convolution_subtract_fusion.6
  193.8 1.7 convolution_add_fusion.7
  195.4 1.7 convolution_subtract_fusion.6
  197.2 1.7 convolution_add_fusion.7
  199.9 1.5 fusion.35
  201.4 1.4 convert_multiply_fusion
  202.8 1.1 copy.33
  204.0 3.3 convolution_multiply_fusion.1
  207.3 136.1 %all-gather.3.cloned.1.call-done = f32[256,128,256]{2,1,0:T(8,128)} async-done(((f32[4,128,256]{2,1,0:T(8,128)}), f32[256,128,256]{2,1,0:T(8,128)}) %all-gather.3.cloned.1.call-update) | async-done | bytes 33554448 | tf_op jit(solution)/shard_map/all_gather | solution.py:16
  343.4 118.9 %while.39 = (s32[]{:T(128)}, f32[4,128,256]{2,1,0:T(8,128)S(1)}, s32[]{:T(128)}, f32[64,4,128,256]{3,2,1,0:T(8,128)}) while((s32[]{:T(128)}, f32[4,128,256]{2,1,0:T(8,128)S(1)}, s32[]{:T(128)}, f32[64,4,128,256]{3,2,1,0:T(8,128)}) %tuple.95), condition=%wide.region_5.6_spmd.clone, body=%wide.region_4.5_spmd.sunk.clone | while | flops 201654272 | bytes 5242947 | solution.py:23
  345.2 1.1 dynamic-slice_bitcast_fusion.3
  462.3 24.9 %while.40 = (s32[]{:T(128)}, f32[4,128,128]{2,1,0:T(8,128)S(1)}, bf16[4,4,128,128]{3,2,1,0:T(8,128)(2,1)}, f32[4,4]{1,0:T(4,128)S(1)}, f32[4,4,128,128]{2,3,1,0:...) while((s32[]{:T(128)}, f32[4,128,128]{2,1,0:T(8,128)S(1)}, ...), condition=%wide.region_8.9_spmd.clone, body=%wide.region_7.8_spmd.sunk.clone | while | flops 402980864 | bytes 3941533 | solution.py:121
  462.3 1.3 convolution_multiply_fusion.5
  463.7 1.4 convolution_subtract_fusion.7
  465.1 2.0 fusion.119
  467.1 1.4 convolution_add_fusion.8
  468.6 1.3 convolution_multiply_fusion.5
  469.9 1.4 convolution_subtract_fusion.7
  471.3 2.0 fusion.119
  473.4 1.4 convolution_add_fusion.8
  474.8 1.3 convolution_multiply_fusion.5
  476.2 1.4 convolution_subtract_fusion.7
  477.6 2.0 fusion.119
  479.6 1.4 convolution_add_fusion.8
  481.0 1.3 convolution_multiply_fusion.5
  482.4 1.4 convolution_subtract_fusion.7
  483.8 2.0 fusion.119
  485.8 1.4 convolution_add_fusion.8
  487.2 1.5 copy.34
  488.7 3.2 fusion.41
  491.9 48.4 %reduce-scatter.2.cloned.1.call-done = f32[128,2048]{1,0:T(8,128)} async-done(((f32[512,2048]{1,0:T(8,128)}), f32[128,2048]{1,0:T(8,128)}) %reduce-scatter.2.cloned.1.call-update) | async-done | bytes 1048592 | tf_op jit(solution)/shard_map/reduce_scatter | solution.py:127
  540.3 2.1 convert_element_type.35
  (298 shorter events, 118.7 us)
Async XLA Ops:
  6.5 482.1 %copy-start = (bf16[512,2048]{1,0:T(8,128)(2,1)S(1)}, bf16[512,2048]{1,0:T(8,128)(2,1)}, u32[]{:S(2)}) copy-start(bf16[512,2048]{1,0:T(8,128)(2,1)} %param.17) | copy-start | bytes 6291460
  6.5 6.3 %copy-start.7 = (f32[4,512]{1,0:T(4,128)S(1)}, f32[4,512]{1,0:T(4,128)}, u32[]{:S(2)}) copy-start(f32[4,512]{1,0:T(4,128)} %param.15) | copy-start | bytes 24580
  6.5 336.8 %all-gather.3.cloned.1.call-start = ((), (), s32[]{:S(2)}) async-start(), calls=%async_computation.2 | async-start | bytes 34078720 | tf_op jit(solution)/shard_map/all_gather | solution.py:16
  12.7 163.6 %copy-start.3 = (f32[512,4,128]{2,0,1:T(8,128)}, f32[512,4,128]{2,0,1:T(8,128)S(1)}, u32[]{:S(2)}) copy-start(f32[512,4,128]{2,0,1:T(8,128)S(1)} %convert_multiply_fusion.2) | copy-start | bytes 3145732
  176.0 1.9 copy-start.6
  181.1 1.0 copy-start.2
  181.1 2.6 copy-start.5
  198.9 0.8 copy-start.1
  199.7 340.6 %reduce-scatter.2.cloned.1.call-start = ((), (), s32[]{:S(2)}) async-start(), calls=%async_computation.1 | async-start | bytes 5242880 | tf_op jit(solution)/shard_map/reduce_scatter | solution.py:127
  199.9 4.0 copy-start.4
Sparse Core Ops, SparseCore 0:
  199.8 143.5 all-gather.2
  492.0 48.2 reduce-scatter.1
where the time goes:
time: 554 us; the launch traced here: 549 us
  waiting for transfers between devices  185 us (33%)
  other arithmetic  183 us (33%)
  matrix products  87.1 us (16%)
  local copies, waits for them, and re-layouts  78 us (14%)
  between operations  13.6 us (2%)
    another operation x4, other arithmetic, prepare(): lax.linalg.triangular_solve(unit_lower, right_sides, left_side=True, lowe...  159 us
    all_gather x1, waiting for transfers between devices, prefix_2(): pieces = lax.all_gather(value, axis)  136 us
    dot_general x89, matrix products, contract(): return jnp.einsum(pattern, left_side, right_side, precision=EXACT)  81.9 us
    squeeze x63, local copies, waits for them, and re-layouts, step(): longer = join(total, pieces[position])  68 us
    reduce_scatter x1, waiting for transfers between devices, body(): lax.psum_scatter(jnp.dot(attended, out_weight, preferred_element_type=jnp...  48.4 us
  transfers between devices with their start and end apart: 2, of which 2 were waited for; matrix products, arithmetic and copies ran while one was open for 1% of the time, Pallas kernels for 0%

commit v1 on v0

v1 whole, which is shorter than its diff:
```python
import jax
import jax.numpy as jnp
from jax import lax
from jax.experimental import pallas as pl
from jax.experimental.pallas import tpu as pltpu
from jax.sharding import PartitionSpec as P

C = 128
LEVELS = (2, 4, 8, 16, 32, 64)
F32, BF16 = jnp.float32, jnp.bfloat16


def dot(a, b):
    return jnp.dot(a, b, preferred_element_type=F32)


def dot_nt(a, b, precision=None):
    return lax.dot_general(a, b, (((1,), (1,)), ((), ())), precision=precision, preferred_element_type=F32)


def halves(a):
    hi = a.astype(BF16)
    return hi, (a - hi.astype(F32)).astype(BF16)


def wide(a, b):
    return jnp.concatenate([a, b], axis=1)


def tall(a, b):
    return jnp.concatenate([a, b], axis=0)


def exact_square(a_halves, b_halves):
    row = wide(*b_halves)
    both = dot(wide(*a_halves), tall(row, row))
    return both[:, :C] + both[:, C:]


def exact_apply(a_halves, b_hi, b_lo):
    return dot(wide(*a_halves), tall(b_hi, b_hi)) + dot(a_halves[0], b_lo)


def fill_masks(masks):
    row = lax.broadcasted_iota(jnp.int32, (C, C), 0)
    col = lax.broadcasted_iota(jnp.int32, (C, C), 1)
    for i, s in enumerate((1,) + LEVELS):
        same = (row // (2 * s)) == (col // (2 * s))
        low = ((row // s) % 2 == 1) & ((col // s) % 2 == 0)
        masks[i] = jnp.where(same & low, 1.0, 0.0).astype(BF16)


def chunk_start(q, k, b_col, g_row, g_col):
    row = lax.broadcasted_iota(jnp.int32, (C, C), 0)
    col = lax.broadcasted_iota(jnp.int32, (C, C), 1)
    eye = row == col
    both = dot_nt(tall(k, q), k)
    gram, query_key = both[:C], both[C:]
    diagonal = jnp.where(eye, gram, 0.0)
    rk_row = lax.rsqrt(jnp.sum(diagonal, axis=0, keepdims=True) + 1e-06)
    rk_col = lax.rsqrt(jnp.sum(diagonal, axis=1, keepdims=True) + 1e-06)
    decay = jnp.exp(jnp.where(row >= col, g_col - g_row, -1e30)) * rk_row
    lower = jnp.where(row > col, decay * gram, 0.0) * (b_col * rk_col)
    return lower, (decay * query_key).astype(BF16), rk_row, rk_col


def invert(lowers, masks):
    row = lax.broadcasted_iota(jnp.int32, (C, C), 0)
    col = lax.broadcasted_iota(jnp.int32, (C, C), 1)
    split = [halves(a) for a in lowers]
    first = masks[0].astype(F32)
    xs = [jnp.where(row == col, 1.0, 0.0) - a * first for a in lowers]
    for i in range(len(LEVELS)):
        mask = masks[i + 1]
        xh = [halves(x) for x in xs]
        ys = [exact_square((hi * mask, lo * mask), x) for (hi, lo), x in zip(split, xh)]
        yh = [halves(y) for y in ys]
        zs = [exact_square(x, y) for x, y in zip(xh, yh)]
        xs = [x - z for x, z in zip(xs, zs)]
    return xs


def chunk_end(x, qkd, q, k, v, b_row, g_row, g_col, rk_row, rk_col):
    row = lax.broadcasted_iota(jnp.int32, (C, C), 0)
    col = lax.broadcasted_iota(jnp.int32, (C, C), 1)
    carried = dot(wide(*halves(x * b_row)), tall(v, v))
    key_factor = dot(wide(*halves(x * (b_row * jnp.exp(g_row) * rk_row))), tall(k, k))
    pair = wide(-key_factor, carried)
    g_end = g_col[C - 1 :, :]
    pair_hi, pair_lo = halves(pair * (jnp.exp(g_end - g_col) * rk_col))
    kt = k.T
    ab = dot(wide(kt, kt), tall(pair_hi, pair_lo))
    step = ab[:, :C] + jnp.where(row == col, jnp.exp(g_end), 0.0)
    added = ab[:, C:]
    qf = q.astype(F32)
    rq_col = lax.rsqrt(jnp.sum(qf * qf, axis=1, keepdims=True) + 1e-06)
    qo = dot(qkd, pair.astype(BF16))
    rows_q = (qo[:, :C] + jnp.exp(g_col) * qf) * rq_col
    rows_o = qo[:, C:] * rq_col
    return step, added, rows_q, rows_o


def head_parts(q_of, k_of, v_of, beta, decay_log, masks, put):
    row = lax.broadcasted_iota(jnp.int32, (C, C), 0)
    col = lax.broadcasted_iota(jnp.int32, (C, C), 1)
    sums = jnp.where(row <= col, 1.0, 0.0)
    logs = jnp.maximum(decay_log, -110.0)
    logs = tall(logs, logs)
    g = jnp.dot(logs, sums, precision=lax.Precision.HIGHEST, preferred_element_type=F32)
    stacked = tall(beta, g[:4])
    turned = stacked.T
    b_row = [beta[c : c + 1] for c in range(4)]
    b_col = [turned[:, c : c + 1] for c in range(4)]
    g_row = [g[c : c + 1] for c in range(4)]
    g_col = [turned[:, 4 + c : 5 + c] for c in range(4)]
    starts = [chunk_start(q_of(c), k_of(c), b_col[c], g_row[c], g_col[c]) for c in range(4)]
    xs = invert([s[0] for s in starts], masks)
    ends = [chunk_end(xs[c], starts[c][1], q_of(c), k_of(c), v_of(c), b_row[c], g_row[c], g_col[c], *starts[c][2:])
            for c in range(4)]
    state = None
    for c in range(4):
        step, added, rows_q, rows_o = ends[c]
        if state is None:
            state = wide(step, added)
        else:
            s_hi, s_lo = halves(state)
            moved = dot(rows_q.astype(BF16), s_hi)
            rows_q = moved[:, :C]
            rows_o = rows_o + moved[:, C:]
            state = exact_apply(halves(step), s_hi, s_lo) + wide(jnp.zeros((C, C), F32), added)
        put(c, rows_q, rows_o)
    return state


def k1_kernel(q_ref, k_ref, v_ref, b_ref, d_ref, qe_ref, o_ref, item_ref, masks):
    h = pl.program_id(0)

    @pl.when(h == 0)
    def _():
        fill_masks(masks)

    def four(ref):
        lines = lax.broadcasted_iota(jnp.int32, (4, 512), 0)
        mine = jnp.sum(jnp.where(lines == h, ref[...], 0.0), axis=0, keepdims=True)
        return jnp.concatenate([mine[:, c * C : (c + 1) * C] for c in range(4)], axis=0)

    def at(ref):
        return lambda c: ref[0, c * C : (c + 1) * C, :]

    def put(c, rows_q, rows_o):
        qe_ref[0, c * C : (c + 1) * C, :] = rows_q.astype(BF16)
        o_ref[0, c * C : (c + 1) * C, :] = rows_o

    state = head_parts(at(q_ref), at(k_ref), at(v_ref), four(b_ref), four(d_ref), masks, put)
    hi, lo = halves(state[:, :C])
    item_ref[0, :, :C] = hi
    item_ref[0, :, C : 2 * C] = lo
    item_ref[0, :, 2 * C :] = state[:, C:].astype(BF16)


def k1(q, k, v, b, d):
    spec = pl.BlockSpec((1, 512, 128), lambda h: (h, 0, 0))
    small = pl.BlockSpec((4, 512), lambda h: (0, 0))
    return pl.pallas_call(
        k1_kernel,
        grid=(4,),
        in_specs=[spec, spec, spec, small, small],
        out_specs=[spec, spec, pl.BlockSpec((1, 128, 384), lambda h: (h, 0, 0))],
        out_shape=[jax.ShapeDtypeStruct((4, 512, 128), BF16), jax.ShapeDtypeStruct((4, 512, 128), F32),
                   jax.ShapeDtypeStruct((4, 128, 384), BF16)],
        scratch_shapes=[pltpu.VMEM((7, C, C), BF16)],
        compiler_params=pltpu.CompilerParams(vmem_limit_bytes=48 * 2**20),
    )(q, k, v, b, d)


MESH = pl.DeviceIdType.MESH


def wide3(hi, lo, u):
    return jnp.concatenate([hi, lo, u], axis=1)


def as_item(state):
    hi, lo = halves(state[:, :C])
    return wide3(hi, lo, state[:, C:].astype(BF16))


def from_item(item):
    return wide(item[:, :C].astype(F32) + item[:, C : 2 * C].astype(F32), item[:, 2 * C :].astype(F32))


def join(later, earlier):
    hi, lo = halves(earlier)
    item_halves = (later[:, :C], later[:, C : 2 * C])
    return exact_apply(item_halves, hi, lo) + wide(jnp.zeros((C, C), F32), later[:, 2 * C :].astype(F32))


def pass_state(item, state):
    s = state.astype(BF16)
    return dot(item[:, : 2 * C], tall(s, s)) + item[:, 2 * C :].astype(F32)


def mix_kernel(item_ref, qe_ref, o_ref, w_ref, out_ref, group, pairs, rows, enters, entering, att, arrived, weight,
               total, state, w_sem, g_send, g_recv, p_send, p_recv, x_send, x_recv, e_send, e_recv, y_send, y_recv):
    seq, head = lax.axis_index("seq"), lax.axis_index("head")
    member, pair, line = seq % 4, (seq // 4) % 4, seq // 16
    base = seq - member

    def in_pairs(step):
        return line * 16 + ((pair + step + 4) % 4) * 4 + member

    barrier = pltpu.get_barrier_semaphore()
    friends = [{"seq": base + (member ^ j)} for j in (1, 2, 3)]
    friends += [{"seq": in_pairs(1)}, {"seq": in_pairs(-1)}]
    friends += [{"seq": (seq + 16 * j) % 64} for j in (1, 2, 3)]
    friends += [{"head": (head + j) % 4} for j in (1, 2, 3)]
    for friend in friends:
        pl.semaphore_signal(barrier, inc=1, device_id=friend, device_id_type=MESH)
    load = pltpu.make_async_copy(w_ref, weight, w_sem)
    load.start()
    pl.semaphore_wait(barrier, len(friends))

    def send(source, target, send_sem, recv_sem, to):
        copy = pltpu.make_async_remote_copy(source, target, send_sem, recv_sem, device_id=to, device_id_type=MESH)
        copy.start()
        return copy

    to_group = []
    for j in (1, 2, 3):
        other = member ^ j
        to_group.append(send(item_ref.at[other], group.at[member], g_send.at[j], g_recv.at[j], {"seq": base + other}))
    group[pl.ds(member, 1)] = item_ref[pl.ds(member, 1)]
    for copy in to_group:
        copy.wait()
    early = join(group[1], from_item(group[0]))
    late = as_item(join(group[3], from_item(group[2])))
    pairs[0] = as_item(join(late, early))

    up = send(pairs.at[0], pairs.at[3], p_send.at[0], p_recv.at[0], {"seq": in_pairs(1)})
    down = send(pairs.at[0], pairs.at[1], p_send.at[1], p_recv.at[1], {"seq": in_pairs(-1)})
    up.wait_recv()
    up2 = send(pairs.at[3, :64], pairs.at[2, :64], p_send.at[2], p_recv.at[2], {"seq": in_pairs(1)})
    down.wait_recv()
    down2 = send(pairs.at[1, 64:], pairs.at[2, 64:], p_send.at[3], p_recv.at[3], {"seq": in_pairs(-1)})
    up.wait_send()
    down.wait_send()
    up2.wait()
    down2.wait()
    eye = jnp.where(
        lax.broadcasted_iota(jnp.int32, (C, 2 * C), 0) == lax.broadcasted_iota(jnp.int32, (C, 2 * C), 1), 1.0, 0.0)
    run = from_item(pairs[(4 - pair) % 4])
    before = jnp.where(pair == 0, eye, run)
    for j in (1, 2, 3):
        run = join(pairs[(j + 4 - pair) % 4], run)
        if j < 3:
            before = jnp.where(pair > j, run, before)

    rows[pl.ds(line, 1)] = run.astype(BF16)[None]
    for j in (1, 2, 3):
        @pl.when(line + j < 4)
        def _():
            send(rows.at[line], rows.at[line], x_send.at[j], x_recv.at[j], {"seq": seq + 16 * j})

    def line_copy(j):
        return pltpu.make_async_remote_copy(rows.at[line], rows.at[line], x_send.at[j], x_recv.at[j],
                                            device_id={"seq": (seq + 16 * j) % 64}, device_id_type=MESH)

    state[...] = jnp.zeros((C, C), F32)
    for j in (3, 2, 1):
        @pl.when(line - j >= 0)
        def _():
            line_copy(j).wait_recv()
            there = rows[line - j]
            state[...] = dot(there[:, :C], state[...].astype(BF16)) + there[:, C:].astype(F32)

    entry = dot(wide(*halves(before[:, :C])), tall(state[...].astype(BF16), state[...].astype(BF16))) + before[:, C:]
    for i in range(4):
        enters[i] = entry.astype(BF16)
        if i < 3:
            entry = pass_state(group[i], entry)
    to_members = []
    for j in (1, 2, 3):
        other = member ^ j
        to_members.append(
            send(enters.at[other], entering.at[member], e_send.at[j], e_recv.at[j], {"seq": base + other}))
    entering[pl.ds(member, 1)] = enters[pl.ds(member, 1)]
    for j in (1, 2, 3):
        @pl.when(line + j < 4)
        def _():
            line_copy(j).wait_send()
    for copy in to_members:
        copy.wait()

    for h in range(4):
        mine = dot(qe_ref[h], entering[h]) + o_ref[h]
        for t in range(4):
            att[t, :, h * C : (h + 1) * C] = mine[t * C : (t + 1) * C].astype(BF16)
    over = []
    for j in (1, 2, 3):
        other = (head + j) % 4
        over.append(send(att.at[other], arrived.at[j], y_send.at[j], y_recv.at[j], {"head": other}))
    load.wait()
    for n in range(4):
        cols = slice(n * 512, (n + 1) * 512)
        total[:, cols] = dot(att[head], weight[head, :, cols])
    for j in (1, 3, 2):
        over[j - 1].wait()
        for n in range(4):
            cols = slice(n * 512, (n + 1) * 512)
            more = total[:, cols] + dot(arrived[j], weight[(head + 4 - j) % 4, :, cols])
            if j == 2:
                out_ref[:, cols] = more.astype(BF16)
            else:
                total[:, cols] = more


def mix(item, qe, o, w):
    vmem = pl.BlockSpec(memory_space=pltpu.VMEM)
    dma = pltpu.SemaphoreType.DMA((4,))
    return pl.pallas_call(
        mix_kernel,
        out_shape=jax.ShapeDtypeStruct((128, 2048), BF16),
        in_specs=[vmem, vmem, vmem, pl.BlockSpec(memory_space=pl.ANY)],
        out_specs=vmem,
        scratch_shapes=[
            pltpu.VMEM((4, C, 3 * C), BF16),
            pltpu.VMEM((4, C, 3 * C), BF16),
            pltpu.VMEM((4, C, 2 * C), BF16),
            pltpu.VMEM((4, C, C), BF16),
            pltpu.VMEM((4, C, C), BF16),
            pltpu.VMEM((4, C, 512), BF16),
            pltpu.VMEM((4, C, 512), BF16),
            pltpu.VMEM((4, 512, 2048), BF16),
            pltpu.VMEM((C, 2048), F32),
            pltpu.VMEM((C, C), F32),
            pltpu.SemaphoreType.DMA,
        ] + [dma] * 10,
        compiler_params=pltpu.CompilerParams(
            collective_id=0, has_side_effects=True, vmem_limit_bytes=48 * 2**20),
    )(item, qe, o, w)


def body(query, key, value, beta, log_decay, out_weight):
    weight = lax.all_gather(out_weight, "head")
    turn = lambda a: a.transpose(1, 0, 2)
    qe, o, item = k1(turn(query), turn(key), turn(value), beta, log_decay)
    return mix(item, qe, o, weight)


def solution(mesh):
    in_specs = (
        P("seq", "head", None),
        P("seq", "head", None),
        P("seq", "head", None),
        P("head", "seq"),
        P("head", "seq"),
        P("head", None),
    )
    out_specs = P(("seq", "head"), None)
    return jax.shard_map(body, mesh=mesh, in_specs=in_specs, out_specs=out_specs, check_vma=False)
```

time: 554 us -> 146 us (0.26)
  other arithmetic: 183 us -> 0 us
  waiting for transfers between devices: 185 us -> 70 us
  matrix products: 87.1 us -> 0 us
  local copies, waits for them, and re-layouts: 78 us -> 4.64 us
  Pallas kernels: 0 us -> 57.9 us
    another operation x5 -> x0, other arithmetic: 161 us -> none  [the longest x4 159 us: prepare(): lax.linalg.triangular_solve(unit_lower, right_sides, left_side=True, lowe...]
    dot_general x90 -> x0, matrix products: 85.1 us -> none  [the longest x89 81.9 us: contract(): return jnp.einsum(pattern, left_side, right_side, precision=EXACT)]
    squeeze x63 -> x0, local copies, waits for them, and re-layouts: 68 us -> none  [step(): longer = join(total, pieces[position])]
    all_gather x1, waiting for transfers between devices: 136 us -> 69.3 us  [body(): weight = lax.all_gather(out_weight, 'head')]
    pallas_call x0 -> x2, Pallas kernels: none -> 57.9 us  [the longest x1 40.6 us: mix(): pl.pallas_call(mix_kernel, out_shape=jax.ShapeDtypeStruct((128, 2048), BF...]
    reduce_scatter x1 -> x0, waiting for transfers between devices: 48.4 us -> none  [body(): lax.psum_scatter(jnp.dot(attended, out_weight, preferred_element_type=jnp...]
    select_n x63 -> x0, other arithmetic: 8.16 us -> none  [step(): return jnp.where(position < mine, longer, total)]
  transfers between devices with their start and end apart: 2 -> 1, of which waited for: 2 -> 1; matrix products, arithmetic and copies ran while one was open for 1% -> 2% of each run, Pallas kernels for 0% -> 12%
where the time goes in v1:
time: 146 us
  waiting for transfers between devices  70 us (48%)
  Pallas kernels  57.9 us (40%)
  between operations  13.4 us (9%)
  local copies, waits for them, and re-layouts  4.64 us (3%)
    all_gather x1, waiting for transfers between devices, body(): weight = lax.all_gather(out_weight, 'head')  69.3 us
    pallas_call x1, Pallas kernels, mix(): pl.pallas_call(mix_kernel, out_shape=jax.ShapeDtypeStruct((128, 2048), BF...  40.6 us
    pallas_call x1, Pallas kernels, k1(): pl.pallas_call(k1_kernel, grid=(4,), in_specs=[spec, spec, spec, small, s...  17.4 us
    unnamed x6, local copies, waits for them, and re-layouts  3.3 us
  transfers between devices with their start and end apart: 1, of which 1 were waited for; matrix products, arithmetic and copies ran while one was open for 2% of the time, Pallas kernels for 12%

profile of v1, /device:TPU:6, one launch (start us, length us, event | category | flops | bytes accessed | tf_op | source)
XLA Modules:
  0.0 146.0 jit_solution(4203492733664918624)
XLA Ops:
  6.5 0.0 all-gather.3.cloned.1.call-start
  6.5 0.7 all-gather.3.cloned.1.call-update
  7.3 1.1 copy.13
  8.4 1.3 copy_bitcast_fusion
  9.7 0.0 copy-start
  9.7 0.7 copy-done
  10.4 0.0 copy-start.1
  10.4 0.7 copy-done.1
  11.1 17.4 %shard_map.64 = (bf16[4,512,128]{2,1,0:T(8,128)(2,1)S(1)}, f32[4,512,128]{2,1,0:T(8,128)S(1)}, bf16[4,128,384]{2,1,0:T(8,128)(2,1)S(1)}) custom-call(bf16[4,512,128]{2,1,0:T(8,128)(2,1)S(1)} %bitcast.8, bf16[4,512,128]{2,1,0:T(8,128)(2,1)S(1)} %get-tuple-element.12.k_ref, bf16[4,512,128]{2,1,0:T(8,128)(2,1)S(1)} %get-tuple-element.11.v_ref, ...), custom_call_target="tpu_custom_call" | custom-call | tf_op jit(solution)/shard_map/pallas_call | solution.py:164
  28.5 69.3 %all-gather.3.cloned.1.call-done = bf16[2048,2048]{1,0:T(8,128)(2,1)} async-done(((bf16[512,2048]{1,0:T(8,128)(2,1)}), bf16[2048,2048]{1,0:T(8,128)(2,1)}) %all-gather.3.cloned.1.call-update) | async-done | bytes 8388624 | tf_op jit(solution)/shard_map/all_gather | solution.py:344
  97.8 40.6 %shard_map.65 = bf16[128,2048]{1,0:T(8,128)(2,1)S(1)} custom-call(bf16[4,128,384]{2,1,0:T(8,128)(2,1)S(1)} %get-tuple-element.8.item_ref, bf16[4,512,128]{2,1,0:T(8,128)(2,1)S(1)} %get-tuple-element.9.qe_ref, f32[4,512,128]{2,1,0:T(8,128)S(1)} %get-tuple-element.10.o_ref, bf16[4,512,2048]{2,1,0:T(8,128)(2,1)} %bitcast.9), custom_call_target="tpu_custom_call" | custom-call | tf_op jit(solution)/shard_map/pallas_call | solution.py:320
  138.4 0.8 copy.15
Async XLA Ops:
  6.5 91.3 %all-gather.3.cloned.1.call-start = ((), (), s32[]{:S(2)}) async-start(), calls=%async_computation | async-start | bytes 10485760 | tf_op jit(solution)/shard_map/all_gather | solution.py:344
  9.7 0.7 copy-start
  10.4 0.7 copy-start.1
Sparse Core Ops, SparseCore 0:
  9.2 88.6 all-gather.2

commit v2 on v1

v2 whole, which is shorter than its diff:
```python
import jax
import jax.numpy as jnp
from jax import lax
from jax.experimental import pallas as pl
from jax.experimental.pallas import tpu as pltpu
from jax.sharding import PartitionSpec as P

C = 128
LEVELS = (2, 4, 8, 16, 32, 64)
F32, BF16 = jnp.float32, jnp.bfloat16


def dot(a, b):
    return jnp.dot(a, b, preferred_element_type=F32)


def dot_nt(a, b, precision=None):
    return lax.dot_general(a, b, (((1,), (1,)), ((), ())), precision=precision, preferred_element_type=F32)


def halves(a):
    hi = a.astype(BF16)
    return hi, (a - hi.astype(F32)).astype(BF16)


def wide(a, b):
    return jnp.concatenate([a, b], axis=1)


def tall(a, b):
    return jnp.concatenate([a, b], axis=0)


def exact_square(a_halves, b_halves):
    row = wide(*b_halves)
    both = dot(wide(*a_halves), tall(row, row))
    return both[:, :C] + both[:, C:]


def exact_apply(a_halves, b_hi, b_lo):
    return dot(wide(*a_halves), tall(b_hi, b_hi)) + dot(a_halves[0], b_lo)


def fill_masks(masks):
    row = lax.broadcasted_iota(jnp.int32, (C, C), 0)
    col = lax.broadcasted_iota(jnp.int32, (C, C), 1)
    for i, s in enumerate((1,) + LEVELS):
        same = (row // (2 * s)) == (col // (2 * s))
        low = ((row // s) % 2 == 1) & ((col // s) % 2 == 0)
        masks[i] = jnp.where(same & low, 1.0, 0.0).astype(BF16)


def chunk_start(q, k, b_col, g_row, g_col):
    row = lax.broadcasted_iota(jnp.int32, (C, C), 0)
    col = lax.broadcasted_iota(jnp.int32, (C, C), 1)
    eye = row == col
    both = dot_nt(tall(k, q), k)
    gram, query_key = both[:C], both[C:]
    diagonal = jnp.where(eye, gram, 0.0)
    rk_row = lax.rsqrt(jnp.sum(diagonal, axis=0, keepdims=True) + 1e-06)
    rk_col = lax.rsqrt(jnp.sum(diagonal, axis=1, keepdims=True) + 1e-06)
    decay = jnp.exp(jnp.where(row >= col, g_col - g_row, -1e30)) * rk_row
    lower = jnp.where(row > col, decay * gram, 0.0) * (b_col * rk_col)
    return lower, (decay * query_key).astype(BF16), rk_row, rk_col


def invert(lowers, masks):
    row = lax.broadcasted_iota(jnp.int32, (C, C), 0)
    col = lax.broadcasted_iota(jnp.int32, (C, C), 1)
    split = [halves(a) for a in lowers]
    first = masks[0].astype(F32)
    xs = [jnp.where(row == col, 1.0, 0.0) - a * first for a in lowers]
    for i in range(len(LEVELS)):
        mask = masks[i + 1]
        xh = [halves(x) for x in xs]
        ys = [exact_square((hi * mask, lo * mask), x) for (hi, lo), x in zip(split, xh)]
        yh = [halves(y) for y in ys]
        zs = [exact_square(x, y) for x, y in zip(xh, yh)]
        xs = [x - z for x, z in zip(xs, zs)]
    return xs


def chunk_end(x, qkd, q, k, v, b_row, g_row, g_col, rk_row, rk_col):
    row = lax.broadcasted_iota(jnp.int32, (C, C), 0)
    col = lax.broadcasted_iota(jnp.int32, (C, C), 1)
    carried = dot(wide(*halves(x * b_row)), tall(v, v))
    key_factor = dot(wide(*halves(x * (b_row * jnp.exp(g_row) * rk_row))), tall(k, k))
    pair = wide(-key_factor, carried)
    g_end = g_col[C - 1 :, :]
    pair_hi, pair_lo = halves(pair * (jnp.exp(g_end - g_col) * rk_col))
    kt = k.T
    ab = dot(wide(kt, kt), tall(pair_hi, pair_lo))
    step = ab[:, :C] + jnp.where(row == col, jnp.exp(g_end), 0.0)
    added = ab[:, C:]
    qf = q.astype(F32)
    rq_col = lax.rsqrt(jnp.sum(qf * qf, axis=1, keepdims=True) + 1e-06)
    qo = dot(qkd, pair.astype(BF16))
    rows_q = (qo[:, :C] + jnp.exp(g_col) * qf) * rq_col
    rows_o = qo[:, C:] * rq_col
    return step, added, rows_q, rows_o


def head_parts(q_of, k_of, v_of, beta, decay_log, masks, put):
    row = lax.broadcasted_iota(jnp.int32, (C, C), 0)
    col = lax.broadcasted_iota(jnp.int32, (C, C), 1)
    sums = jnp.where(row <= col, 1.0, 0.0)
    logs = jnp.maximum(decay_log, -110.0)
    logs = tall(logs, logs)
    g = jnp.dot(logs, sums, precision=lax.Precision.HIGHEST, preferred_element_type=F32)
    stacked = tall(beta, g[:4])
    turned = stacked.T
    b_row = [beta[c : c + 1] for c in range(4)]
    b_col = [turned[:, c : c + 1] for c in range(4)]
    g_row = [g[c : c + 1] for c in range(4)]
    g_col = [turned[:, 4 + c : 5 + c] for c in range(4)]
    starts = [chunk_start(q_of(c), k_of(c), b_col[c], g_row[c], g_col[c]) for c in range(4)]
    xs = invert([s[0] for s in starts], masks)
    ends = [chunk_end(xs[c], starts[c][1], q_of(c), k_of(c), v_of(c), b_row[c], g_row[c], g_col[c], *starts[c][2:])
            for c in range(4)]
    state = None
    for c in range(4):
        step, added, rows_q, rows_o = ends[c]
        if state is None:
            state = wide(step, added)
        else:
            s_hi, s_lo = halves(state)
            moved = dot(rows_q.astype(BF16), s_hi)
            rows_q = moved[:, :C]
            rows_o = rows_o + moved[:, C:]
            state = exact_apply(halves(step), s_hi, s_lo) + wide(jnp.zeros((C, C), F32), added)
        put(c, rows_q, rows_o)
    return state


MESH = pl.DeviceIdType.MESH


def as_item(state):
    hi, lo = halves(state[:, :C])
    return jnp.concatenate([hi, lo, state[:, C:].astype(BF16)], axis=1)


def from_item(item):
    return wide(item[:, :C].astype(F32) + item[:, C : 2 * C].astype(F32), item[:, 2 * C :].astype(F32))


def join(later, earlier):
    hi, lo = halves(earlier)
    return exact_apply((later[:, :C], later[:, C : 2 * C]), hi, lo) + wide(
        jnp.zeros((C, C), F32), later[:, 2 * C :].astype(F32))


def pass_state(item, state):
    return exact_square((item[:, :C], item[:, C : 2 * C]), halves(state)) + item[:, 2 * C :].astype(F32)


def layer_kernel(q_ref, k_ref, v_ref, b_ref, d_ref, w_ref, out_ref,
                 masks, qe, own, items, group, pairs, rows, enters, entering, att, arrived, weight, total, state,
                 w_load, w_send, w_recv, g_send, g_recv, p_send, p_recv, x_send, x_recv, e_send, e_recv,
                 y_send, y_recv):
    seq, head = lax.axis_index("seq"), lax.axis_index("head")
    member, pair, line = seq % 4, (seq // 4) % 4, seq // 16
    core = seq % 2
    base = seq - member
    right, left, across = (head + 1) % 4, (head + 3) % 4, (head + 2) % 4

    def in_pairs(step):
        return line * 16 + ((pair + step) % 4) * 4 + member

    barrier = pltpu.get_barrier_semaphore()
    friends = [{"seq": base + (member ^ j)} for j in (1, 2, 3)]
    friends += [{"seq": in_pairs(j)} for j in (1, 2, 3)]
    friends += [{"seq": (seq + 16 * j) % 64} for j in (1, 2, 3)]
    friends += [{"head": (head + j) % 4} for j in (1, 2, 3)]
    for friend in friends:
        pl.semaphore_signal(barrier, inc=1, device_id=friend, device_id_type=MESH)
    load = pltpu.make_async_copy(w_ref, weight.at[head], w_load)
    load.start()
    fill_masks(masks)
    load.wait()
    pl.semaphore_wait(barrier, len(friends))

    def copy_to(source, target, send_sem, recv_sem, to):
        return pltpu.make_async_remote_copy(source, target, send_sem, recv_sem, device_id=to, device_id_type=MESH)

    def quarter(of, part):
        return weight.at[of, 2 * core + part]

    sibling = {"seq": seq ^ 1}
    to_right, to_left = {"head": right}, {"head": left}
    ra = lambda of: copy_to(quarter(of, 0), quarter(of, 0), w_send.at[0], w_recv.at[0], to_right)
    lb = lambda of: copy_to(quarter(of, 1), quarter(of, 1), w_send.at[1], w_recv.at[1], to_left)
    rb = lambda of: copy_to(quarter(of, 1), quarter(of, 1), w_send.at[2], w_recv.at[2], to_right)
    la = lambda of: copy_to(quarter(of, 0), quarter(of, 0), w_send.at[3], w_recv.at[3], to_left)
    ra2 = lambda of: copy_to(quarter(of, 0), quarter(of, 0), w_send.at[4], w_recv.at[4], to_right)
    lb2 = lambda of: copy_to(quarter(of, 1), quarter(of, 1), w_send.at[5], w_recv.at[5], to_left)

    def over(of, part, i):
        return copy_to(quarter(of, part), quarter(of, part), w_send.at[6 + i], w_recv.at[6 + i], sibling)

    ra(head).start()
    lb(head).start()
    rb(head).start()
    la(head).start()

    def item_copy(h):
        return copy_to(items.at[h], group.at[member], g_send.at[h], g_recv.at[member], {"seq": base + h})

    def pair_copy(j):
        return copy_to(pairs.at[0], pairs.at[4 - j], p_send.at[j], p_recv.at[j], {"seq": in_pairs(j)})

    def line_copy(j):
        return copy_to(rows.at[line], rows.at[line], x_send.at[j], x_recv.at[j], {"seq": (seq + 16 * j) % 64})

    def from_group():
        for j in (1, 2, 3):
            other = member ^ j
            copy_to(group.at[other], group.at[other], g_send.at[other], g_recv.at[other],
                    {"seq": base + other}).wait_recv()
        early = join(group[1], from_item(group[0]))
        late = as_item(join(group[3], from_item(group[2])))
        pairs[0] = as_item(join(late, early))
        for j in (1, 3, 2):
            pair_copy(j).start()

    def one_head(h, _):
        def four(ref):
            lines = lax.broadcasted_iota(jnp.int32, (4, 512), 0)
            mine = jnp.sum(jnp.where(lines == h, ref[...], 0.0), axis=0, keepdims=True)
            return jnp.concatenate([mine[:, c * C : (c + 1) * C] for c in range(4)], axis=0)

        def at(ref):
            return lambda c: ref[h, c * C : (c + 1) * C, :]

        def put(c, rows_q, rows_o):
            qe[h, c * C : (c + 1) * C, :] = rows_q.astype(BF16)
            own[h, c * C : (c + 1) * C, :] = rows_o

        items[h] = as_item(head_parts(at(q_ref), at(k_ref), at(v_ref), four(b_ref), four(d_ref), masks, put))

        @pl.when(h != member)
        def _():
            item_copy(h).start()

        @pl.when(h == member)
        def _():
            group[h] = items[h]

        @pl.when((h == member + 1) & (h < 3))
        def _():
            from_group()

        @pl.when(h == 2)
        def _():
            ra(left).wait_recv()
            ra2(left).start()
            lb(right).wait_recv()
            lb2(right).start()
            over(left, 0, 0).start()
            over(right, 1, 1).start()

        return 0

    lax.fori_loop(0, 4, one_head, 0)

    @pl.when(member >= 2)
    def _():
        from_group()

    for j in (1, 3, 2):
        pair_copy(j).wait_recv()
    eye = jnp.where(
        lax.broadcasted_iota(jnp.int32, (C, 2 * C), 0) == lax.broadcasted_iota(jnp.int32, (C, 2 * C), 1), 1.0, 0.0)
    run = from_item(pairs[(4 - pair) % 4])
    before = jnp.where(pair == 0, eye, run)
    for j in (1, 2, 3):
        run = join(pairs[(j + 4 - pair) % 4], run)
        if j < 3:
            before = jnp.where(pair > j, run, before)

    rows[line] = as_item(run)
    for j in (1, 2, 3):
        @pl.when(line + j < 4)
        def _():
            line_copy(j).start()

    rb(left).wait_recv()
    over(left, 1, 2).start()
    la(right).wait_recv()
    over(right, 0, 3).start()
    state[...] = jnp.zeros((C, C), F32)
    for j in (3, 2, 1):
        @pl.when(line - j >= 0)
        def _():
            line_copy(j).wait_recv()
            state[...] = pass_state(rows[line - j], state[...])

    entry = exact_square(halves(before[:, :C]), halves(state[...])) + before[:, C:]
    for i in range(4):
        enters[i] = entry.astype(BF16)
        if i < 3:
            entry = pass_state(group[i], entry)

    def enter_copy(j):
        other = member ^ j
        return copy_to(enters.at[other], entering.at[member], e_send.at[other], e_recv.at[member],
                       {"seq": base + other})

    for j in (1, 2, 3):
        enter_copy(j).start()
    entering[member] = enters[member]

    def out_copy(p, j):
        return copy_to(att.at[p, (head + j) % 4], arrived.at[p, j], y_send.at[p, j], y_recv.at[p, j],
                       {"head": (head + j) % 4})

    for h in range(4):
        @pl.when(member != h)
        def _():
            copy_to(entering.at[h], entering.at[h], e_send.at[h], e_recv.at[h], {"seq": base + h}).wait_recv()
        mine = dot(qe[h], entering[h]) + own[h]
        for t in range(4):
            att[h // 2, t, :, (h % 2) * C : (h % 2 + 1) * C] = mine[t * C : (t + 1) * C].astype(BF16)
        if h % 2 == 1:
            for j in (2, 1, 3):
                out_copy(h // 2, j).start()

    ra2(across).wait_recv()
    over(across, 0, 4).start()
    lb2(across).wait_recv()
    over(across, 1, 5).start()
    ra(head).wait_send()
    lb(head).wait_send()
    rb(head).wait_send()
    la(head).wait_send()
    ra2(left).wait_send()
    lb2(right).wait_send()

    def other_half(of, part):
        return weight.at[of, 2 * (1 - core) + part]

    for i, (of, part) in enumerate(((left, 0), (right, 1), (left, 1), (right, 0), (across, 0), (across, 1))):
        over(of, part, i).wait_send()
        copy_to(other_half(of, part), other_half(of, part), w_send.at[6 + i], w_recv.at[6 + i], sibling).wait_recv()
    for j in (1, 2, 3):
        item_copy(member ^ j).wait_send()
        pair_copy(j).wait_send()
        enter_copy(j).wait_send()

        @pl.when(line + j < 4)
        def _():
            line_copy(j).wait_send()

    def product(left_side, of, p, cols):
        w = jnp.concatenate([weight[of, 2 * p, :, cols], weight[of, 2 * p + 1, :, cols]], axis=0)
        return dot(left_side, w)

    for p in range(2):
        for j in (0, 1, 3, 2):
            if j:
                out_copy(p, j).wait()
            for n in range(4):
                cols = slice(n * 512, (n + 1) * 512)
                part = att[p, head] if j == 0 else arrived[p, j]
                more = product(part, (head + 4 - j) % 4, p, cols)
                if p or j:
                    more = total[:, cols] + more
                if p == 1 and j == 2:
                    out_ref[:, cols] = more.astype(BF16)
                else:
                    total[:, cols] = more


def layer(q, k, v, b, d, w):
    vmem = pl.BlockSpec(memory_space=pltpu.VMEM)
    dma = pltpu.SemaphoreType.DMA
    return pl.pallas_call(
        layer_kernel,
        out_shape=jax.ShapeDtypeStruct((128, 2048), BF16),
        in_specs=[vmem] * 5 + [pl.BlockSpec(memory_space=pl.ANY)],
        out_specs=vmem,
        scratch_shapes=[
            pltpu.VMEM((7, C, C), BF16),
            pltpu.VMEM((4, 512, C), BF16),
            pltpu.VMEM((4, 512, C), F32),
            pltpu.VMEM((4, C, 3 * C), BF16),
            pltpu.VMEM((4, C, 3 * C), BF16),
            pltpu.VMEM((4, C, 3 * C), BF16),
            pltpu.VMEM((4, C, 3 * C), BF16),
            pltpu.VMEM((4, C, C), BF16),
            pltpu.VMEM((4, C, C), BF16),
            pltpu.VMEM((2, 4, C, 2 * C), BF16),
            pltpu.VMEM((2, 4, C, 2 * C), BF16),
            pltpu.VMEM((4, 4, C, 2048), BF16),
            pltpu.VMEM((C, 2048), F32),
            pltpu.VMEM((C, C), F32),
            dma, dma((12,)), dma((12,)),
        ] + [dma((4,))] * 8 + [dma((2, 4))] * 2,
        compiler_params=pltpu.CompilerParams(
            collective_id=0, has_side_effects=True, vmem_limit_bytes=56 * 2**20),
    )(q, k, v, b, d, w)


def body(query, key, value, beta, log_decay, out_weight):
    turn = lambda a: a.transpose(1, 0, 2)
    return layer(turn(query), turn(key), turn(value), beta, log_decay, out_weight.reshape(4, C, 2048))


def solution(mesh):
    in_specs = (
        P("seq", "head", None),
        P("seq", "head", None),
        P("seq", "head", None),
        P("head", "seq"),
        P("head", "seq"),
        P("head", None),
    )
    out_specs = P(("seq", "head"), None)
    return jax.shard_map(body, mesh=mesh, in_specs=in_specs, out_specs=out_specs, check_vma=False)
```

time: 146 us -> 62 us (0.42)
  waiting for transfers between devices: 70 us -> 0 us
  between operations: 13.4 us -> 0.01 us
  Pallas kernels: 57.9 us -> 55.2 us
  local copies, waits for them, and re-layouts: 4.64 us -> 6.11 us
    all_gather x1 -> x0, waiting for transfers between devices: 69.3 us -> none  [body(): weight = lax.all_gather(out_weight, 'head')]
    pallas_call x2 -> x1, Pallas kernels: 57.9 us -> 55.2 us  [layer(): pl.pallas_call(layer_kernel, out_shape=jax.ShapeDtypeStruct((128, 2048),...]
    unnamed x6 -> x2, local copies, waits for them, and re-layouts: 3.3 us -> 3.78 us
  transfers between devices with their start and end apart: 1 -> 0, of which waited for: 1 -> 0; matrix products, arithmetic and copies ran while one was open for 2% -> 0% of each run, Pallas kernels for 12% -> 0%
where the time goes in v2:
time: 62 us; the launch traced here: 61.4 us
  Pallas kernels  55.2 us (89%)
  local copies, waits for them, and re-layouts  6.11 us (10%)
    pallas_call x1, Pallas kernels, layer(): pl.pallas_call(layer_kernel, out_shape=jax.ShapeDtypeStruct((128, 2048),...  55.2 us
    unnamed x2, local copies, waits for them, and re-layouts  3.78 us
    transpose x1, local copies, waits for them, and re-layouts, body(): turn = lambda a: a.transpose(1, 0, 2)  2.32 us

profile of v2, /device:TPU:6, one launch (start us, length us, event | category | flops | bytes accessed | tf_op | source)
XLA Modules:
  0.0 61.4 jit_solution(12732085299711732004)
XLA Ops:
  0.0 1.9 %copy.13 = bf16[512,4,128]{2,0,1:T(8,128)(2,1)} copy(bf16[512,4,128]{2,1,0:T(4,128)(2,1)} %param.6) | data formatting | bytes 1048576 | tf_op args[0]
  1.9 2.3 %copy_bitcast_fusion = (bf16[4,512,128]{2,1,0:T(8,128)(2,1)}, bf16[4,512,128]{2,1,0:T(8,128)(2,1)}) fusion(bf16[512,4,128]{2,1,0:T(4,128)(2,1)} %param.8, bf16[512,4,128]{2,1,0:T(4,128)(2,1)} %param.7), kind=kLoop, calls=%fused_computation | loop fusion | bytes 2097152 | tf_op jit(solution)/shard_map/transpose | solution.py:405
  4.2 55.2 %shard_map.64 = bf16[128,2048]{1,0:T(8,128)(2,1)} custom-call(bf16[4,512,128]{2,1,0:T(8,128)(2,1)} %bitcast.9, bf16[4,512,128]{2,1,0:T(8,128)(2,1)} %get-tuple-element.6.k_ref, bf16[4,512,128]{2,1,0:T(8,128)(2,1)} %get-tuple-element.5.v_ref, f32[4,512]{1,0:T(4,128)} %b_ref.1, f32[4,512]{1,0:T(4,128)} %d_ref.1, bf16[4,128,2048]{2,1,0:T(8,128)(2,1)} %bitcast.8), custom_call_target="tpu_custom_call" | custom-call | tf_op jit(solution)/shard_map/pallas_call | solution.py:377
  59.5 1.9 %copy.15 = bf16[128,2048]{1,0:T(8,128)(2,1)} copy(bf16[128,2048]{1,0:T(8,128)(2,1)} %shard_map.64) | data formatting | bytes 1048576

commit v3 on v2

--- a/solution.py
+++ b/solution.py
@@ -44,10 +44,9 @@
 def fill_masks(masks):
     row = lax.broadcasted_iota(jnp.int32, (C, C), 0)
     col = lax.broadcasted_iota(jnp.int32, (C, C), 1)
+    apart = jnp.where(row > col, row ^ col, 0)
     for i, s in enumerate((1,) + LEVELS):
-        same = (row // (2 * s)) == (col // (2 * s))
-        low = ((row // s) % 2 == 1) & ((col // s) % 2 == 0)
-        masks[i] = jnp.where(same & low, 1.0, 0.0).astype(BF16)
+        masks[i] = jnp.where((apart >= s) & (apart < 2 * s), 1.0, 0.0).astype(BF16)
 
 
 def chunk_start(q, k, b_col, g_row, g_col):
@@ -61,7 +60,7 @@
     rk_col = lax.rsqrt(jnp.sum(diagonal, axis=1, keepdims=True) + 1e-06)
     decay = jnp.exp(jnp.where(row >= col, g_col - g_row, -1e30)) * rk_row
     lower = jnp.where(row > col, decay * gram, 0.0) * (b_col * rk_col)
-    return lower, (decay * query_key).astype(BF16), rk_row, rk_col
+    return lower, halves(decay * query_key), rk_row, rk_col
 
 
 def invert(lowers, masks):
@@ -94,7 +93,7 @@
     added = ab[:, C:]
     qf = q.astype(F32)
     rq_col = lax.rsqrt(jnp.sum(qf * qf, axis=1, keepdims=True) + 1e-06)
-    qo = dot(qkd, pair.astype(BF16))
+    qo = exact_apply(qkd, *halves(pair))
     rows_q = (qo[:, :C] + jnp.exp(g_col) * qf) * rq_col
     rows_o = qo[:, C:] * rq_col
     return step, added, rows_q, rows_o
@@ -124,7 +123,7 @@
             state = wide(step, added)
         else:
             s_hi, s_lo = halves(state)
-            moved = dot(rows_q.astype(BF16), s_hi)
+            moved = exact_apply(halves(rows_q), s_hi, s_lo)
             rows_q = moved[:, :C]
             rows_o = rows_o + moved[:, C:]
             state = exact_apply(halves(step), s_hi, s_lo) + wide(jnp.zeros((C, C), F32), added)
@@ -154,9 +153,10 @@
     return exact_square((item[:, :C], item[:, C : 2 * C]), halves(state)) + item[:, 2 * C :].astype(F32)
 
 
-def layer_kernel(q_ref, k_ref, v_ref, b_ref, d_ref, w_ref, out_ref,
-                 masks, qe, own, items, group, pairs, rows, enters, entering, att, arrived, weight, total, state,
-                 w_load, w_send, w_recv, g_send, g_recv, p_send, p_recv, x_send, x_recv, e_send, e_recv,
+def layer_kernel(q_in, k_in, v_in, b_in, d_in, w_ref, out_ref,
+                 q_ref, k_ref, v_ref, b_ref, d_ref, masks, qs, ks, vs, qe, own, items, group, pairs, rows, enters, entering, att, arrived, weight,
+                 total, prefix, state,
+                 in_load, w_load, w_send, w_recv, g_send, g_recv, p_send, p_recv, x_send, x_recv, e_send, e_recv,
                  y_send, y_recv):
     seq, head = lax.axis_index("seq"), lax.axis_index("head")
     member, pair, line = seq % 4, (seq // 4) % 4, seq // 16
@@ -176,7 +176,15 @@
         pl.semaphore_signal(barrier, inc=1, device_id=friend, device_id_type=MESH)
     load = pltpu.make_async_copy(w_ref, weight.at[head], w_load)
     load.start()
+    loads = [pltpu.make_async_copy(source, target, in_load.at[i]) for i, (source, target) in enumerate(
+        ((q_in, q_ref), (k_in, k_ref), (v_in, v_ref), (b_in, b_ref), (d_in, d_ref)))]
+    for copy in loads:
+        copy.start()
     fill_masks(masks)
+    for copy in loads:
+        copy.wait()
+    for source, target in ((q_ref, qs), (k_ref, ks), (v_ref, vs)):
+        target[...] = source[...].astype(F32).reshape(2048, C)
     load.wait()
     pl.semaphore_wait(barrier, len(friends))
 
@@ -212,7 +220,39 @@
     def line_copy(j):
         return copy_to(rows.at[line], rows.at[line], x_send.at[j], x_recv.at[j], {"seq": (seq + 16 * j) % 64})
 
-    def from_group():
+    def enter_copy(j):
+        other = member ^ j
+        return copy_to(enters.at[other], entering.at[member], e_send.at[other], e_recv.at[member],
+                       {"seq": base + other})
+
+    def out_copy(h, j):
+        return copy_to(att.at[(head + j) % 4, h], arrived.at[j, h], y_send.at[j, h], y_recv.at[j, h],
+                       {"head": (head + j) % 4})
+
+    def compute(h):
+        def four(ref):
+            lines = lax.broadcasted_iota(jnp.int32, (4, 512), 0)
+            mine = jnp.sum(jnp.where(lines == h, ref[...], 0.0), axis=0, keepdims=True)
+            return jnp.concatenate([mine[:, c * C : (c + 1) * C] for c in range(4)], axis=0)
+
+        def at(ref):
+            return lambda c: ref[pl.ds(c * 512 + h, C, stride=4), :].astype(BF16)
+
+        def put(c, rows_q, rows_o):
+            qe[h, c * C : (c + 1) * C, :] = rows_q.astype(BF16)
+            own[h, c * C : (c + 1) * C, :] = rows_o
+
+        items[h] = as_item(head_parts(at(qs), at(ks), at(vs), four(b_ref), four(d_ref), masks, put))
+
+        @pl.when(h != member)
+        def _():
+            item_copy(h).start()
+
+        @pl.when(h == member)
+        def _():
+            group[h] = items[h]
+
+    def scan_group():
         for j in (1, 2, 3):
             other = member ^ j
             copy_to(group.at[other], group.at[other], g_send.at[other], g_recv.at[other],
@@ -220,35 +260,71 @@
         early = join(group[1], from_item(group[0]))
         late = as_item(join(group[3], from_item(group[2])))
         pairs[0] = as_item(join(late, early))
+        for j in (2, 1, 3):
+            pair_copy(j).start()
+
+    def scan_pairs():
         for j in (1, 3, 2):
-            pair_copy(j).start()
-
-    def one_head(h, _):
-        def four(ref):
-            lines = lax.broadcasted_iota(jnp.int32, (4, 512), 0)
-            mine = jnp.sum(jnp.where(lines == h, ref[...], 0.0), axis=0, keepdims=True)
-            return jnp.concatenate([mine[:, c * C : (c + 1) * C] for c in range(4)], axis=0)
-
-        def at(ref):
-            return lambda c: ref[h, c * C : (c + 1) * C, :]
-
-        def put(c, rows_q, rows_o):
-            qe[h, c * C : (c + 1) * C, :] = rows_q.astype(BF16)
-            own[h, c * C : (c + 1) * C, :] = rows_o
-
-        items[h] = as_item(head_parts(at(q_ref), at(k_ref), at(v_ref), four(b_ref), four(d_ref), masks, put))
-
-        @pl.when(h != member)
-        def _():
-            item_copy(h).start()
-
-        @pl.when(h == member)
-        def _():
-            group[h] = items[h]
-
-        @pl.when((h == member + 1) & (h < 3))
-        def _():
-            from_group()
+            pair_copy(j).wait_recv()
+        eye = jnp.where(
+            lax.broadcasted_iota(jnp.int32, (C, 2 * C), 0) == lax.broadcasted_iota(jnp.int32, (C, 2 * C), 1), 1.0, 0.0)
+        run = from_item(pairs[(4 - pair) % 4])
+        before = jnp.where(pair == 0, eye, run)
+        for j in (1, 2, 3):
+            run = join(pairs[(j + 4 - pair) % 4], run)
+            if j < 3:
+                before = jnp.where(pair > j, run, before)
+        rows[line] = as_item(run)
+        for j in (2, 1, 3):
+            @pl.when(line + j < 4)
+            def _():
+                line_copy(j).start()
+        prefix[...] = before
+
+    def scan_lines():
+        state[...] = jnp.zeros((C, C), F32)
+        for j in (3, 2, 1):
+            @pl.when(line - j >= 0)
+            def _():
+                line_copy(j).wait_recv()
+                state[...] = pass_state(rows[line - j], state[...])
+
+        before = prefix[...]
+        entry = exact_square(halves(before[:, :C]), halves(state[...])) + before[:, C:]
+        for i in range(4):
+            enters[i] = entry.astype(BF16)
+            if i < 3:
+                entry = pass_state(group[i], entry)
+        for j in (1, 2, 3):
+            enter_copy(j).start()
+        entering[member] = enters[member]
+
+    def apply(h):
+        @pl.when(member != h)
+        def _():
+            copy_to(entering.at[h], entering.at[h], e_send.at[h], e_recv.at[h], {"seq": base + h}).wait_recv()
+        mine = dot(qe[h], entering[h]) + own[h]
+        for t in range(4):
+            att[t, h] = mine[t * C : (t + 1) * C].astype(BF16)
+        for j in (2, 1, 3):
+            out_copy(h, j).start()
+
+    def step(h, _):
+        @pl.when(h < 4)
+        def _():
+            compute(h)
+
+        @pl.when(h == member + 1)
+        def _():
+            scan_group()
+
+        @pl.when(h == member + 2)
+        def _():
+            scan_pairs()
+
+        @pl.when(h == member + 3)
+        def _():
+            scan_lines()
 
         @pl.when(h == 2)
         def _():
@@ -259,71 +335,21 @@
             over(left, 0, 0).start()
             over(right, 1, 1).start()
 
+        @pl.when(h == 5)
+        def _():
+            rb(left).wait_recv()
+            over(left, 1, 2).start()
+            la(right).wait_recv()
+            over(right, 0, 3).start()
+
+        @pl.when(h >= 4)
+        def _():
+            apply(h - 4)
+
         return 0
 
-    lax.fori_loop(0, 4, one_head, 0)
-
-    @pl.when(member >= 2)
-    def _():
-        from_group()
-
-    for j in (1, 3, 2):
-        pair_copy(j).wait_recv()
-    eye = jnp.where(
-        lax.broadcasted_iota(jnp.int32, (C, 2 * C), 0) == lax.broadcasted_iota(jnp.int32, (C, 2 * C), 1), 1.0, 0.0)
-    run = from_item(pairs[(4 - pair) % 4])
-    before = jnp.where(pair == 0, eye, run)
-    for j in (1, 2, 3):
-        run = join(pairs[(j + 4 - pair) % 4], run)
-        if j < 3:
-            before = jnp.where(pair > j, run, before)
-
-    rows[line] = as_item(run)
-    for j in (1, 2, 3):
-        @pl.when(line + j < 4)
-        def _():
-            line_copy(j).start()
-
-    rb(left).wait_recv()
-    over(left, 1, 2).start()
-    la(right).wait_recv()
-    over(right, 0, 3).start()
-    state[...] = jnp.zeros((C, C), F32)
-    for j in (3, 2, 1):
-        @pl.when(line - j >= 0)
-        def _():
-            line_copy(j).wait_recv()
-            state[...] = pass_state(rows[line - j], state[...])
-
-    entry = exact_square(halves(before[:, :C]), halves(state[...])) + before[:, C:]
-    for i in range(4):
-        enters[i] = entry.astype(BF16)
-        if i < 3:
-            entry = pass_state(group[i], entry)
-
-    def enter_copy(j):
-        other = member ^ j
-        return copy_to(enters.at[other], entering.at[member], e_send.at[other], e_recv.at[member],
-                       {"seq": base + other})
-
-    for j in (1, 2, 3):
-        enter_copy(j).start()
-    entering[member] = enters[member]
-
-    def out_copy(p, j):
-        return copy_to(att.at[p, (head + j) % 4], arrived.at[p, j], y_send.at[p, j], y_recv.at[p, j],
-                       {"head": (head + j) % 4})
-
-    for h in range(4):
-        @pl.when(member != h)
-        def _():
-            copy_to(entering.at[h], entering.at[h], e_send.at[h], e_recv.at[h], {"seq": base + h}).wait_recv()
-        mine = dot(qe[h], entering[h]) + own[h]
-        for t in range(4):
-            att[h // 2, t, :, (h % 2) * C : (h % 2 + 1) * C] = mine[t * C : (t + 1) * C].astype(BF16)
-        if h % 2 == 1:
-            for j in (2, 1, 3):
-                out_copy(h // 2, j).start()
+    lax.fori_loop(0, 7, step, 0)
+    apply(3)
 
     ra2(across).wait_recv()
     over(across, 0, 4).start()
@@ -335,13 +361,6 @@
     la(head).wait_send()
     ra2(left).wait_send()
     lb2(right).wait_send()
-
-    def other_half(of, part):
-        return weight.at[of, 2 * (1 - core) + part]
-
-    for i, (of, part) in enumerate(((left, 0), (right, 1), (left, 1), (right, 0), (across, 0), (across, 1))):
-        over(of, part, i).wait_send()
-        copy_to(other_half(of, part), other_half(of, part), w_send.at[6 + i], w_recv.at[6 + i], sibling).wait_recv()
     for j in (1, 2, 3):
         item_copy(member ^ j).wait_send()
         pair_copy(j).wait_send()
@@ -351,24 +370,30 @@
         def _():
             line_copy(j).wait_send()
 
-    def product(left_side, of, p, cols):
-        w = jnp.concatenate([weight[of, 2 * p, :, cols], weight[of, 2 * p + 1, :, cols]], axis=0)
-        return dot(left_side, w)
-
-    for p in range(2):
-        for j in (0, 1, 3, 2):
-            if j:
-                out_copy(p, j).wait()
-            for n in range(4):
-                cols = slice(n * 512, (n + 1) * 512)
-                part = att[p, head] if j == 0 else arrived[p, j]
-                more = product(part, (head + 4 - j) % 4, p, cols)
-                if p or j:
-                    more = total[:, cols] + more
-                if p == 1 and j == 2:
-                    out_ref[:, cols] = more.astype(BF16)
-                else:
-                    total[:, cols] = more
+    def other_half(of, part):
+        return weight.at[of, 2 * (1 - core) + part]
+
+    for i, (of, part) in enumerate(((left, 0), (right, 1), (left, 1), (right, 0), (across, 0), (across, 1))):
+        over(of, part, i).wait_send()
+        copy_to(other_half(of, part), other_half(of, part), w_send.at[6 + i], w_recv.at[6 + i], sibling).wait_recv()
+
+    def product(heads, cols):
+        rows_in = jnp.concatenate(
+            [att[head, h] if j == 0 else arrived[j, h] for j in range(4) for h in heads], axis=1)
+        rows_w = jnp.concatenate(
+            [weight[(head + 4 - j) % 4, h, :, cols] for j in range(4) for h in heads], axis=0)
+        return dot(rows_in, rows_w)
+
+    for h in range(3):
+        for j in (1, 3, 2):
+            out_copy(h, j).wait()
+    for n in range(4):
+        total[:, n * 512 : (n + 1) * 512] = product((0, 1, 2), slice(n * 512, (n + 1) * 512))
+    for j in (1, 3, 2):
+        out_copy(3, j).wait()
+    for n in range(4):
+        cols = slice(n * 512, (n + 1) * 512)
+        out_ref[:, cols] = (total[:, cols] + product((3,), cols)).astype(BF16)
 
 
 def layer(q, k, v, b, d, w):
@@ -377,10 +402,13 @@
     return pl.pallas_call(
         layer_kernel,
         out_shape=jax.ShapeDtypeStruct((128, 2048), BF16),
-        in_specs=[vmem] * 5 + [pl.BlockSpec(memory_space=pl.ANY)],
+        in_specs=[pl.BlockSpec(memory_space=pltpu.HBM)] * 6,
         out_specs=vmem,
-        scratch_shapes=[
+        scratch_shapes=[pltpu.VMEM((512, 4, C), BF16)] * 3 + [pltpu.VMEM((4, 512), F32)] * 2 + [
             pltpu.VMEM((7, C, C), BF16),
+            pltpu.VMEM((2048, C), F32),
+            pltpu.VMEM((2048, C), F32),
+            pltpu.VMEM((2048, C), F32),
             pltpu.VMEM((4, 512, C), BF16),
             pltpu.VMEM((4, 512, C), F32),
             pltpu.VMEM((4, C, 3 * C), BF16),
@@ -389,21 +417,22 @@
             pltpu.VMEM((4, C, 3 * C), BF16),
             pltpu.VMEM((4, C, C), BF16),
             pltpu.VMEM((4, C, C), BF16),
-            pltpu.VMEM((2, 4, C, 2 * C), BF16),
-            pltpu.VMEM((2, 4, C, 2 * C), BF16),
+            pltpu.VMEM((4, 4, C, C), BF16),
+            pltpu.VMEM((4, 4, C, C), BF16),
             pltpu.VMEM((4, 4, C, 2048), BF16),
             pltpu.VMEM((C, 2048), F32),
+            pltpu.VMEM((C, 2 * C), F32),
             pltpu.VMEM((C, C), F32),
-            dma, dma((12,)), dma((12,)),
-        ] + [dma((4,))] * 8 + [dma((2, 4))] * 2,
+            dma((5,)), dma, dma((12,)), dma((12,)),
+        ] + [dma((4,))] * 8 + [dma((4, 4))] * 2,
         compiler_params=pltpu.CompilerParams(
-            collective_id=0, has_side_effects=True, vmem_limit_bytes=56 * 2**20),
+            collective_id=0, has_side_effects=True, vmem_limit_bytes=28 * 2**20),
     )(q, k, v, b, d, w)
 
 
 def body(query, key, value, beta, log_decay, out_weight):
-    turn = lambda a: a.transpose(1, 0, 2)
-    return layer(turn(query), turn(key), turn(value), beta, log_decay, out_weight.reshape(4, C, 2048))
+    stay = lambda a: pltpu.with_memory_space_constraint(a, pltpu.HBM)
+    return layer(stay(query), stay(key), stay(value), stay(beta), stay(log_decay), stay(out_weight.reshape(4, C, 2048)))
 
 
 def solution(mesh):

time: 62 us -> 55.7 us (0.90)
  local copies, waits for them, and re-layouts: 6.11 us -> 0.8 us
    unnamed x2 -> x1, local copies, waits for them, and re-layouts: 3.78 us -> 0.8 us
    transpose x1 -> x0, local copies, waits for them, and re-layouts: 2.32 us -> none  [body(): turn = lambda a: a.transpose(1, 0, 2)]
    pallas_call x1, Pallas kernels: 55.2 us -> 54.6 us  [layer(): pl.pallas_call(layer_kernel, out_shape=jax.ShapeDtypeStruct((128, 2048),...]
where the time goes in v3:
time: 55.7 us; the launch traced here: 55.4 us
  Pallas kernels  54.6 us (98%)
  local copies, waits for them, and re-layouts  0.8 us (1%)
    pallas_call x1, Pallas kernels, layer(): pl.pallas_call(layer_kernel, out_shape=jax.ShapeDtypeStruct((128, 2048),...  54.6 us

profile of v3, /device:TPU:6, one launch (start us, length us, event | category | flops | bytes accessed | tf_op | source)
XLA Modules:
  0.0 55.4 jit_solution(10535461182731115729)
XLA Ops:
  0.0 54.6 %shard_map.64 = bf16[128,2048]{1,0:T(8,128)(2,1)S(1)} custom-call(bf16[512,4,128]{2,1,0:T(4,128)(2,1)} %q_in.1, bf16[512,4,128]{2,1,0:T(4,128)(2,1)} %k_in.1, bf16[512,4,128]{2,1,0:T(4,128)(2,1)} %v_in.1, f32[4,512]{1,0:T(4,128)} %b_in.1, f32[4,512]{1,0:T(4,128)} %d_in.1, bf16[4,128,2048]{2,1,0:T(8,128)(2,1)} %bitcast.1), custom_call_target="tpu_custom_call" | custom-call | tf_op jit(solution)/shard_map/pallas_call | solution.py:402
  54.6 0.8 %copy.8 = bf16[128,2048]{1,0:T(8,128)(2,1)} copy(bf16[128,2048]{1,0:T(8,128)(2,1)S(1)} %shard_map.64) | data formatting | bytes 1048576

commit v4 on v3

--- a/solution.py
+++ b/solution.py
@@ -49,18 +49,16 @@
         masks[i] = jnp.where((apart >= s) & (apart < 2 * s), 1.0, 0.0).astype(BF16)
 
 
-def chunk_start(q, k, b_col, g_row, g_col):
+def chunk_start(k, b_col, g_row, g_col):
     row = lax.broadcasted_iota(jnp.int32, (C, C), 0)
     col = lax.broadcasted_iota(jnp.int32, (C, C), 1)
-    eye = row == col
-    both = dot_nt(tall(k, q), k)
-    gram, query_key = both[:C], both[C:]
-    diagonal = jnp.where(eye, gram, 0.0)
+    gram = dot_nt(k, k)
+    diagonal = jnp.where(row == col, gram, 0.0)
     rk_row = lax.rsqrt(jnp.sum(diagonal, axis=0, keepdims=True) + 1e-06)
     rk_col = lax.rsqrt(jnp.sum(diagonal, axis=1, keepdims=True) + 1e-06)
     decay = jnp.exp(jnp.where(row >= col, g_col - g_row, -1e30)) * rk_row
     lower = jnp.where(row > col, decay * gram, 0.0) * (b_col * rk_col)
-    return lower, halves(decay * query_key), rk_row, rk_col
+    return lower, decay, rk_row, rk_col
 
 
 def invert(lowers, masks):
@@ -79,7 +77,7 @@
     return xs
 
 
-def chunk_end(x, qkd, q, k, v, b_row, g_row, g_col, rk_row, rk_col):
+def chunk_end(x, k, v, b_row, g_row, g_col, rk_row, rk_col):
     row = lax.broadcasted_iota(jnp.int32, (C, C), 0)
     col = lax.broadcasted_iota(jnp.int32, (C, C), 1)
     carried = dot(wide(*halves(x * b_row)), tall(v, v))
@@ -90,45 +88,47 @@
     kt = k.T
     ab = dot(wide(kt, kt), tall(pair_hi, pair_lo))
     step = ab[:, :C] + jnp.where(row == col, jnp.exp(g_end), 0.0)
-    added = ab[:, C:]
-    qf = q.astype(F32)
-    rq_col = lax.rsqrt(jnp.sum(qf * qf, axis=1, keepdims=True) + 1e-06)
-    qo = exact_apply(qkd, *halves(pair))
-    rows_q = (qo[:, :C] + jnp.exp(g_col) * qf) * rq_col
-    rows_o = qo[:, C:] * rq_col
-    return step, added, rows_q, rows_o
-
-
-def head_parts(q_of, k_of, v_of, beta, decay_log, masks, put):
+    return pair, wide(step, ab[:, C:])
+
+
+def compose(later, earlier):
+    return exact_apply(halves(later[:, :C]), *halves(earlier)) + wide(jnp.zeros((C, C), F32), later[:, C:])
+
+
+def key_side(k_of, v_of, beta, decay_log, masks, keep):
     row = lax.broadcasted_iota(jnp.int32, (C, C), 0)
     col = lax.broadcasted_iota(jnp.int32, (C, C), 1)
     sums = jnp.where(row <= col, 1.0, 0.0)
     logs = jnp.maximum(decay_log, -110.0)
     logs = tall(logs, logs)
     g = jnp.dot(logs, sums, precision=lax.Precision.HIGHEST, preferred_element_type=F32)
-    stacked = tall(beta, g[:4])
-    turned = stacked.T
+    turned = tall(beta, g[:4]).T
     b_row = [beta[c : c + 1] for c in range(4)]
     b_col = [turned[:, c : c + 1] for c in range(4)]
     g_row = [g[c : c + 1] for c in range(4)]
     g_col = [turned[:, 4 + c : 5 + c] for c in range(4)]
-    starts = [chunk_start(q_of(c), k_of(c), b_col[c], g_row[c], g_col[c]) for c in range(4)]
+    starts = [chunk_start(k_of(c), b_col[c], g_row[c], g_col[c]) for c in range(4)]
     xs = invert([s[0] for s in starts], masks)
-    ends = [chunk_end(xs[c], starts[c][1], q_of(c), k_of(c), v_of(c), b_row[c], g_row[c], g_col[c], *starts[c][2:])
-            for c in range(4)]
-    state = None
-    for c in range(4):
-        step, added, rows_q, rows_o = ends[c]
-        if state is None:
-            state = wide(step, added)
-        else:
-            s_hi, s_lo = halves(state)
-            moved = exact_apply(halves(rows_q), s_hi, s_lo)
-            rows_q = moved[:, :C]
-            rows_o = rows_o + moved[:, C:]
-            state = exact_apply(halves(step), s_hi, s_lo) + wide(jnp.zeros((C, C), F32), added)
-        put(c, rows_q, rows_o)
-    return state
+    ends = [chunk_end(xs[c], k_of(c), v_of(c), b_row[c], g_row[c], g_col[c], *starts[c][2:]) for c in range(4)]
+    maps = [e[1] for e in ends]
+    two = compose(maps[1], maps[0])
+    other = compose(maps[3], maps[2])
+    three = compose(maps[2], two)
+    for c, before in enumerate((None, maps[0], two, three)):
+        keep(c, starts[c][1], jnp.exp(g_col[c]), ends[c][0], before)
+    return compose(other, two)
+
+
+def query_side(q, k, decay, growth, pair, before):
+    qf = q.astype(F32)
+    rq_col = lax.rsqrt(jnp.sum(qf * qf, axis=1, keepdims=True) + 1e-06)
+    qo = exact_apply(halves(decay * dot_nt(q, k)), *halves(pair))
+    rows_q = (qo[:, :C] + growth * qf) * rq_col
+    rows_o = qo[:, C:] * rq_col
+    if before is None:
+        return rows_q, rows_o
+    moved = exact_apply(halves(rows_q), *halves(before))
+    return moved[:, :C], rows_o + moved[:, C:]
 
 
 MESH = pl.DeviceIdType.MESH
@@ -154,8 +154,8 @@
 
 
 def layer_kernel(q_in, k_in, v_in, b_in, d_in, w_ref, out_ref,
-                 q_ref, k_ref, v_ref, b_ref, d_ref, masks, qs, ks, vs, qe, own, items, group, pairs, rows, enters, entering, att, arrived, weight,
-                 total, prefix, state,
+                 q_ref, k_ref, v_ref, b_ref, d_ref, masks, qs, ks, vs, decays, growths, chunk_pairs, befores, qe, own, items, group, pairs, rows, enters, entering, att, arrived, weight,
+                 total, group_maps, entry_maps, entry_adds, state,
                  in_load, w_load, w_send, w_recv, g_send, g_recv, p_send, p_recv, x_send, x_recv, e_send, e_recv,
                  y_send, y_recv):
     seq, head = lax.axis_index("seq"), lax.axis_index("head")
@@ -174,12 +174,12 @@
     friends += [{"head": (head + j) % 4} for j in (1, 2, 3)]
     for friend in friends:
         pl.semaphore_signal(barrier, inc=1, device_id=friend, device_id_type=MESH)
+    loads = [pltpu.make_async_copy(source, target, in_load.at[i]) for i, (source, target) in enumerate(
+        ((b_in, b_ref), (d_in, d_ref), (k_in, k_ref), (v_in, v_ref), (q_in, q_ref)))]
+    for copy in loads:
+        copy.start()
     load = pltpu.make_async_copy(w_ref, weight.at[head], w_load)
     load.start()
-    loads = [pltpu.make_async_copy(source, target, in_load.at[i]) for i, (source, target) in enumerate(
-        ((q_in, q_ref), (k_in, k_ref), (v_in, v_ref), (b_in, b_ref), (d_in, d_ref)))]
-    for copy in loads:
-        copy.start()
     fill_masks(masks)
     for copy in loads:
         copy.wait()
@@ -229,28 +229,39 @@
         return copy_to(att.at[(head + j) % 4, h], arrived.at[j, h], y_send.at[j, h], y_recv.at[j, h],
                        {"head": (head + j) % 4})
 
+    def at(ref, h):
+        return lambda c: ref[pl.ds(c * 512 + h, C, stride=4), :].astype(BF16)
+
     def compute(h):
         def four(ref):
             lines = lax.broadcasted_iota(jnp.int32, (4, 512), 0)
             mine = jnp.sum(jnp.where(lines == h, ref[...], 0.0), axis=0, keepdims=True)
             return jnp.concatenate([mine[:, c * C : (c + 1) * C] for c in range(4)], axis=0)
 
-        def at(ref):
-            return lambda c: ref[pl.ds(c * 512 + h, C, stride=4), :].astype(BF16)
-
-        def put(c, rows_q, rows_o):
+        def keep(c, decay, growth, pair_here, before):
+            decays[h, c] = decay
+            growths[h, c] = growth
+            chunk_pairs[h, c] = pair_here
+            if c:
+                befores[h, c - 1] = before
+
+        items[h] = as_item(key_side(at(ks, h), at(vs, h), four(b_ref), four(d_ref), masks, keep))
+
+        @pl.when(h != member)
+        def _():
+            item_copy(h).start()
+
+        @pl.when(h == member)
+        def _():
+            group[h] = items[h]
+
+    def compute_rows(h):
+        q_of, k_of = at(qs, h), at(ks, h)
+        for c in range(4):
+            rows_q, rows_o = query_side(q_of(c), k_of(c), decays[h, c], growths[h, c], chunk_pairs[h, c],
+                                        befores[h, c - 1] if c else None)
             qe[h, c * C : (c + 1) * C, :] = rows_q.astype(BF16)
             own[h, c * C : (c + 1) * C, :] = rows_o
-
-        items[h] = as_item(head_parts(at(qs), at(ks), at(vs), four(b_ref), four(d_ref), masks, put))
-
-        @pl.when(h != member)
-        def _():
-            item_copy(h).start()
-
-        @pl.when(h == member)
-        def _():
-            group[h] = items[h]
 
     def scan_group():
         for j in (1, 2, 3):
@@ -262,39 +273,51 @@
         pairs[0] = as_item(join(late, early))
         for j in (2, 1, 3):
             pair_copy(j).start()
+        group_maps[0] = group[0]
+        group_maps[1] = as_item(early)
+        group_maps[2] = as_item(join(group[2], early))
 
     def scan_pairs():
         for j in (1, 3, 2):
             pair_copy(j).wait_recv()
-        eye = jnp.where(
-            lax.broadcasted_iota(jnp.int32, (C, 2 * C), 0) == lax.broadcasted_iota(jnp.int32, (C, 2 * C), 1), 1.0, 0.0)
-        run = from_item(pairs[(4 - pair) % 4])
-        before = jnp.where(pair == 0, eye, run)
-        for j in (1, 2, 3):
-            run = join(pairs[(j + 4 - pair) % 4], run)
-            if j < 3:
-                before = jnp.where(pair > j, run, before)
-        rows[line] = as_item(run)
+        at_pair = [pairs[(j + 4 - pair) % 4] for j in range(4)]
+        first = from_item(at_pair[0])
+        early = join(at_pair[1], first)
+        late = as_item(join(at_pair[3], from_item(at_pair[2])))
+        rows[line] = as_item(join(late, early))
         for j in (2, 1, 3):
             @pl.when(line + j < 4)
             def _():
                 line_copy(j).start()
-        prefix[...] = before
+        eye = jnp.where(
+            lax.broadcasted_iota(jnp.int32, (C, 2 * C), 0) == lax.broadcasted_iota(jnp.int32, (C, 2 * C), 1), 1.0, 0.0)
+        before = jnp.where(pair == 0, eye, first)
+        before = jnp.where(pair > 1, early, before)
+        before = jnp.where(pair > 2, join(at_pair[2], early), before)
+        for i in range(4):
+            here = join(group_maps[i - 1], before) if i else before
+            hi, lo = halves(here[:, :C])
+            entry_maps[i * C : (i + 1) * C, :C] = hi
+            entry_maps[i * C : (i + 1) * C, C:] = lo
+            entry_adds[i * C : (i + 1) * C, :] = here[:, C:]
 
     def scan_lines():
         state[...] = jnp.zeros((C, C), F32)
-        for j in (3, 2, 1):
-            @pl.when(line - j >= 0)
+        for i in range(3):
+            @pl.when(line > i)
             def _():
-                line_copy(j).wait_recv()
-                state[...] = pass_state(rows[line - j], state[...])
-
-        before = prefix[...]
-        entry = exact_square(halves(before[:, :C]), halves(state[...])) + before[:, C:]
+                copy_to(rows.at[i], rows.at[i], x_send.at[line - i], x_recv.at[line - i],
+                        {"seq": (seq + 16) % 64}).wait_recv()
+                if i == 0:
+                    state[...] = rows[0, :, 2 * C :].astype(F32)
+                else:
+                    state[...] = pass_state(rows[i], state[...])
+
+        row = wide(*halves(state[...]))
+        both = dot(entry_maps[...], tall(row, row))
+        all_four = (both[:, :C] + both[:, C:] + entry_adds[...]).astype(BF16)
         for i in range(4):
-            enters[i] = entry.astype(BF16)
-            if i < 3:
-                entry = pass_state(group[i], entry)
+            enters[i] = all_four[i * C : (i + 1) * C]
         for j in (1, 2, 3):
             enter_copy(j).start()
         entering[member] = enters[member]
@@ -310,6 +333,10 @@
             out_copy(h, j).start()
 
     def step(h, _):
+        @pl.when(h >= 4)
+        def _():
+            compute_rows(h - 4)
+
         @pl.when(h < 4)
         def _():
             compute(h)
@@ -326,7 +353,7 @@
         def _():
             scan_lines()
 
-        @pl.when(h == 2)
+        @pl.when(h == 3)
         def _():
             ra(left).wait_recv()
             ra2(left).start()
@@ -349,6 +376,7 @@
         return 0
 
     lax.fori_loop(0, 7, step, 0)
+    compute_rows(3)
     apply(3)
 
     ra2(across).wait_recv()
@@ -409,6 +437,10 @@
             pltpu.VMEM((2048, C), F32),
             pltpu.VMEM((2048, C), F32),
             pltpu.VMEM((2048, C), F32),
+            pltpu.VMEM((4, 4, C, C), F32),
+            pltpu.VMEM((4, 4, C, 1), F32),
+            pltpu.VMEM((4, 4, C, 2 * C), F32),
+            pltpu.VMEM((4, 3, C, 2 * C), F32),
             pltpu.VMEM((4, 512, C), BF16),
             pltpu.VMEM((4, 512, C), F32),
             pltpu.VMEM((4, C, 3 * C), BF16),
@@ -421,12 +453,14 @@
             pltpu.VMEM((4, 4, C, C), BF16),
             pltpu.VMEM((4, 4, C, 2048), BF16),
             pltpu.VMEM((C, 2048), F32),
-            pltpu.VMEM((C, 2 * C), F32),
+            pltpu.VMEM((3, C, 3 * C), BF16),
+            pltpu.VMEM((4 * C, 2 * C), BF16),
+            pltpu.VMEM((4 * C, C), F32),
             pltpu.VMEM((C, C), F32),
             dma((5,)), dma, dma((12,)), dma((12,)),
         ] + [dma((4,))] * 8 + [dma((4, 4))] * 2,
         compiler_params=pltpu.CompilerParams(
-            collective_id=0, has_side_effects=True, vmem_limit_bytes=28 * 2**20),
+            collective_id=0, has_side_effects=True, vmem_limit_bytes=40 * 2**20),
     )(q, k, v, b, d, w)
 
 

time: 55.7 us -> 53.3 us (0.957)
  Pallas kernels: 54.6 us -> 52.4 us
    pallas_call x1, Pallas kernels: 54.6 us -> 52.4 us  [layer(): pl.pallas_call(layer_kernel, out_shape=jax.ShapeDtypeStruct((128, 2048),...]
where the time goes in v4:
time: 53.3 us; the launch traced here: 53.2 us
  Pallas kernels  52.4 us (98%)
  local copies, waits for them, and re-layouts  0.8 us (2%)
    pallas_call x1, Pallas kernels, layer(): pl.pallas_call(layer_kernel, out_shape=jax.ShapeDtypeStruct((128, 2048),...  52.4 us

profile of v4, /device:TPU:6, one launch (start us, length us, event | category | flops | bytes accessed | tf_op | source)
XLA Modules:
  0.0 53.2 jit_solution(14251571976172393540)
XLA Ops:
  0.0 52.4 %shard_map.64 = bf16[128,2048]{1,0:T(8,128)(2,1)S(1)} custom-call(bf16[512,4,128]{2,1,0:T(4,128)(2,1)} %q_in.1, bf16[512,4,128]{2,1,0:T(4,128)(2,1)} %k_in.1, bf16[512,4,128]{2,1,0:T(4,128)(2,1)} %v_in.1, f32[4,512]{1,0:T(4,128)} %b_in.1, f32[4,512]{1,0:T(4,128)} %d_in.1, bf16[4,128,2048]{2,1,0:T(8,128)(2,1)} %bitcast.1), custom_call_target="tpu_custom_call" | custom-call | tf_op jit(solution)/shard_map/pallas_call | solution.py:430
  52.4 0.8 %copy.8 = bf16[128,2048]{1,0:T(8,128)(2,1)} copy(bf16[128,2048]{1,0:T(8,128)(2,1)S(1)} %shard_map.64) | data formatting | bytes 1048576

commit v5 on v4

--- a/solution.py
+++ b/solution.py
@@ -7,6 +7,7 @@
 
 C = 128
 LEVELS = (2, 4, 8, 16, 32, 64)
+MIDDLE = 2
 F32, BF16 = jnp.float32, jnp.bfloat16
 
 
@@ -61,7 +62,7 @@
     return lower, decay, rk_row, rk_col
 
 
-def invert(lowers, masks):
+def invert(lowers, masks, middle):
     row = lax.broadcasted_iota(jnp.int32, (C, C), 0)
     col = lax.broadcasted_iota(jnp.int32, (C, C), 1)
     split = [halves(a) for a in lowers]
@@ -74,6 +75,8 @@
         yh = [halves(y) for y in ys]
         zs = [exact_square(x, y) for x, y in zip(xh, yh)]
         xs = [x - z for x, z in zip(xs, zs)]
+        if i == MIDDLE:
+            middle()
     return xs
 
 
@@ -95,28 +98,32 @@
     return exact_apply(halves(later[:, :C]), *halves(earlier)) + wide(jnp.zeros((C, C), F32), later[:, C:])
 
 
-def key_side(k_of, v_of, beta, decay_log, masks, keep):
+def running_sums(beta, decay_log):
     row = lax.broadcasted_iota(jnp.int32, (C, C), 0)
     col = lax.broadcasted_iota(jnp.int32, (C, C), 1)
     sums = jnp.where(row <= col, 1.0, 0.0)
     logs = jnp.maximum(decay_log, -110.0)
-    logs = tall(logs, logs)
-    g = jnp.dot(logs, sums, precision=lax.Precision.HIGHEST, preferred_element_type=F32)
+    g = jnp.dot(tall(logs, logs), sums, precision=lax.Precision.HIGHEST, preferred_element_type=F32)
     turned = tall(beta, g[:4]).T
-    b_row = [beta[c : c + 1] for c in range(4)]
-    b_col = [turned[:, c : c + 1] for c in range(4)]
-    g_row = [g[c : c + 1] for c in range(4)]
-    g_col = [turned[:, 4 + c : 5 + c] for c in range(4)]
-    starts = [chunk_start(k_of(c), b_col[c], g_row[c], g_col[c]) for c in range(4)]
-    xs = invert([s[0] for s in starts], masks)
-    ends = [chunk_end(xs[c], k_of(c), v_of(c), b_row[c], g_row[c], g_col[c], *starts[c][2:]) for c in range(4)]
-    maps = [e[1] for e in ends]
-    two = compose(maps[1], maps[0])
-    other = compose(maps[3], maps[2])
-    three = compose(maps[2], two)
-    for c, before in enumerate((None, maps[0], two, three)):
-        keep(c, starts[c][1], jnp.exp(g_col[c]), ends[c][0], before)
-    return compose(other, two)
+    return [(beta[c : c + 1], turned[:, c : c + 1], g[c : c + 1], turned[:, 4 + c : 5 + c]) for c in range(4)]
+
+
+def key_side(heads, masks, middle):
+    rates = [running_sums(beta, logs) for _, _, beta, logs, _ in heads]
+    starts = [[chunk_start(head[0](c), *rate[c][1:]) for c in range(4)] for head, rate in zip(heads, rates)]
+    xs = invert([start[0] for four in starts for start in four], masks, middle)
+    results = []
+    for i, (k_of, v_of, _, _, keep) in enumerate(heads):
+        ends = [chunk_end(xs[4 * i + c], k_of(c), v_of(c), rates[i][c][0], *rates[i][c][2:], *starts[i][c][2:])
+                for c in range(4)]
+        maps = [e[1] for e in ends]
+        two = compose(maps[1], maps[0])
+        other = compose(maps[3], maps[2])
+        three = compose(maps[2], two)
+        for c, before in enumerate((None, maps[0], two, three)):
+            keep(c, starts[i][c][1], jnp.exp(rates[i][c][3]), ends[c][0], before)
+        results.append(compose(other, two))
+    return results
 
 
 def query_side(q, k, decay, growth, pair, before):
@@ -181,12 +188,10 @@
     load = pltpu.make_async_copy(w_ref, weight.at[head], w_load)
     load.start()
     fill_masks(masks)
-    for copy in loads:
+    for copy in loads[:4]:
         copy.wait()
-    for source, target in ((q_ref, qs), (k_ref, ks), (v_ref, vs)):
+    for source, target in ((k_ref, ks), (v_ref, vs)):
         target[...] = source[...].astype(F32).reshape(2048, C)
-    load.wait()
-    pl.semaphore_wait(barrier, len(friends))
 
     def copy_to(source, target, send_sem, recv_sem, to):
         return pltpu.make_async_remote_copy(source, target, send_sem, recv_sem, device_id=to, device_id_type=MESH)
@@ -206,10 +211,13 @@
     def over(of, part, i):
         return copy_to(quarter(of, part), quarter(of, part), w_send.at[6 + i], w_recv.at[6 + i], sibling)
 
-    ra(head).start()
-    lb(head).start()
-    rb(head).start()
-    la(head).start()
+    def greet():
+        load.wait()
+        pl.semaphore_wait(barrier, len(friends))
+        ra(head).start()
+        lb(head).start()
+        rb(head).start()
+        la(head).start()
 
     def item_copy(h):
         return copy_to(items.at[h], group.at[member], g_send.at[h], g_recv.at[member], {"seq": base + h})
@@ -232,28 +240,44 @@
     def at(ref, h):
         return lambda c: ref[pl.ds(c * 512 + h, C, stride=4), :].astype(BF16)
 
-    def compute(h):
-        def four(ref):
-            lines = lax.broadcasted_iota(jnp.int32, (4, 512), 0)
-            mine = jnp.sum(jnp.where(lines == h, ref[...], 0.0), axis=0, keepdims=True)
-            return jnp.concatenate([mine[:, c * C : (c + 1) * C] for c in range(4)], axis=0)
-
-        def keep(c, decay, growth, pair_here, before):
-            decays[h, c] = decay
-            growths[h, c] = growth
-            chunk_pairs[h, c] = pair_here
-            if c:
-                befores[h, c - 1] = before
-
-        items[h] = as_item(key_side(at(ks, h), at(vs, h), four(b_ref), four(d_ref), masks, keep))
-
-        @pl.when(h != member)
-        def _():
-            item_copy(h).start()
-
-        @pl.when(h == member)
-        def _():
-            group[h] = items[h]
+    def compute(two):
+        def head_of(h):
+            def four(ref):
+                lines = lax.broadcasted_iota(jnp.int32, (4, 512), 0)
+                mine = jnp.sum(jnp.where(lines == h, ref[...], 0.0), axis=0, keepdims=True)
+                return jnp.concatenate([mine[:, c * C : (c + 1) * C] for c in range(4)], axis=0)
+
+            def keep(c, decay, growth, pair_here, before):
+                decays[h, c] = decay
+                growths[h, c] = growth
+                chunk_pairs[h, c] = pair_here
+                if c:
+                    befores[h, c - 1] = before
+
+            return at(ks, h), at(vs, h), four(b_ref), four(d_ref), keep
+
+        def middle():
+            @pl.when(two == 0)
+            def _():
+                greet()
+
+            @pl.when((two == 1) & (member < 2))
+            def _():
+                scan_group()
+
+        heads = [2 * two, 2 * two + 1]
+        for h, result in zip(heads, key_side([head_of(h) for h in heads], masks, middle)):
+            items[h] = as_item(result)
+
+            @pl.when(h != member)
+            def _():
+                item_copy(h).start()
+
+            @pl.when(h == member)
+            def _():
+                group[h] = items[h]
+
+        return 0
 
     def compute_rows(h):
         q_of, k_of = at(qs, h), at(ks, h)
@@ -332,28 +356,27 @@
         for j in (2, 1, 3):
             out_copy(h, j).start()
 
-    def step(h, _):
-        @pl.when(h >= 4)
-        def _():
-            compute_rows(h - 4)
-
-        @pl.when(h < 4)
-        def _():
-            compute(h)
-
-        @pl.when(h == member + 1)
+    lax.fori_loop(0, 2, lambda two, _: compute(two), 0)
+    loads[4].wait()
+    qs[...] = q_ref[...].astype(F32).reshape(2048, C)
+    late = member // 2
+
+    def step(t, _):
+        compute_rows(t)
+
+        @pl.when((t == 0) & (late == 1))
         def _():
             scan_group()
 
-        @pl.when(h == member + 2)
+        @pl.when(t == late + 1)
         def _():
             scan_pairs()
 
-        @pl.when(h == member + 3)
+        @pl.when(t == late + 2)
         def _():
             scan_lines()
 
-        @pl.when(h == 3)
+        @pl.when(t == 1)
         def _():
             ra(left).wait_recv()
             ra2(left).start()
@@ -362,22 +385,22 @@
             over(left, 0, 0).start()
             over(right, 1, 1).start()
 
-        @pl.when(h == 5)
+        @pl.when(t == 2)
         def _():
             rb(left).wait_recv()
             over(left, 1, 2).start()
             la(right).wait_recv()
             over(right, 0, 3).start()
 
-        @pl.when(h >= 4)
-        def _():
-            apply(h - 4)
-
         return 0
 
-    lax.fori_loop(0, 7, step, 0)
-    compute_rows(3)
-    apply(3)
+    lax.fori_loop(0, 4, step, 0)
+
+    def step_out(h, _):
+        apply(h)
+        return 0
+
+    lax.fori_loop(0, 4, step_out, 0)
 
     ra2(across).wait_recv()
     over(across, 0, 4).start()

time: 53.3 us -> 55.5 us (1.041)
  the two profiles are of different devices: /device:TPU:6 before, /device:TPU:70 now
where the time goes in v5:
time: 55.5 us; the launch traced here: 55.4 us
  Pallas kernels  54.5 us (98%)
  local copies, waits for them, and re-layouts  0.8 us (1%)
    pallas_call x1, Pallas kernels, layer(): pl.pallas_call(layer_kernel, out_shape=jax.ShapeDtypeStruct((128, 2048),...  54.5 us

profile of v5, /device:TPU:70, one launch (start us, length us, event | category | flops | bytes accessed | tf_op | source)
XLA Modules:
  0.0 55.4 jit_solution(14215704154511307385)
XLA Ops:
  0.0 54.5 %shard_map.64 = bf16[128,2048]{1,0:T(8,128)(2,1)S(1)} custom-call(bf16[512,4,128]{2,1,0:T(4,128)(2,1)} %q_in.1, bf16[512,4,128]{2,1,0:T(4,128)(2,1)} %k_in.1, bf16[512,4,128]{2,1,0:T(4,128)(2,1)} %v_in.1, f32[4,512]{1,0:T(4,128)} %b_in.1, f32[4,512]{1,0:T(4,128)} %d_in.1, bf16[4,128,2048]{2,1,0:T(8,128)(2,1)} %bitcast.1), custom_call_target="tpu_custom_call" | custom-call | tf_op jit(solution)/shard_map/pallas_call | solution.py:453
  54.6 0.8 %copy.8 = bf16[128,2048]{1,0:T(8,128)(2,1)} copy(bf16[128,2048]{1,0:T(8,128)(2,1)S(1)} %shard_map.64) | data formatting | bytes 1048576

commit v6 on v5

--- a/solution.py
+++ b/solution.py
@@ -160,6 +160,10 @@
     return exact_square((item[:, :C], item[:, C : 2 * C]), halves(state)) + item[:, 2 * C :].astype(F32)
 
 
+def swapped(i):
+    return (i % 2) * 2 + i // 2
+
+
 def layer_kernel(q_in, k_in, v_in, b_in, d_in, w_ref, out_ref,
                  q_ref, k_ref, v_ref, b_ref, d_ref, masks, qs, ks, vs, decays, growths, chunk_pairs, befores, qe, own, items, group, pairs, rows, enters, entering, att, arrived, weight,
                  total, group_maps, entry_maps, entry_adds, state,
@@ -169,6 +173,8 @@
     member, pair, line = seq % 4, (seq // 4) % 4, seq // 16
     core = seq % 2
     base = seq - member
+    mine = swapped(member)
+    late = mine // 2
     right, left, across = (head + 1) % 4, (head + 3) % 4, (head + 2) % 4
 
     def in_pairs(step):
@@ -220,7 +226,7 @@
         la(head).start()
 
     def item_copy(h):
-        return copy_to(items.at[h], group.at[member], g_send.at[h], g_recv.at[member], {"seq": base + h})
+        return copy_to(items.at[h], group.at[member], g_send.at[h], g_recv.at[member], {"seq": base + swapped(h)})
 
     def pair_copy(j):
         return copy_to(pairs.at[0], pairs.at[4 - j], p_send.at[j], p_recv.at[j], {"seq": in_pairs(j)})
@@ -230,7 +236,7 @@
 
     def enter_copy(j):
         other = member ^ j
-        return copy_to(enters.at[other], entering.at[member], e_send.at[other], e_recv.at[member],
+        return copy_to(enters.at[other], entering.at[mine], e_send.at[other], e_recv.at[mine],
                        {"seq": base + other})
 
     def out_copy(h, j):
@@ -261,7 +267,7 @@
             def _():
                 greet()
 
-            @pl.when((two == 1) & (member < 2))
+            @pl.when((two == 1) & (late == 0))
             def _():
                 scan_group()
 
@@ -269,13 +275,13 @@
         for h, result in zip(heads, key_side([head_of(h) for h in heads], masks, middle)):
             items[h] = as_item(result)
 
-            @pl.when(h != member)
+            @pl.when(h != mine)
             def _():
                 item_copy(h).start()
 
-            @pl.when(h == member)
+            @pl.when(h == mine)
             def _():
-                group[h] = items[h]
+                group[member] = items[h]
 
         return 0
 
@@ -344,25 +350,33 @@
             enters[i] = all_four[i * C : (i + 1) * C]
         for j in (1, 2, 3):
             enter_copy(j).start()
-        entering[member] = enters[member]
+        entering[mine] = enters[member]
 
     def apply(h):
-        @pl.when(member != h)
-        def _():
-            copy_to(entering.at[h], entering.at[h], e_send.at[h], e_recv.at[h], {"seq": base + h}).wait_recv()
-        mine = dot(qe[h], entering[h]) + own[h]
+        @pl.when(mine != h)
+        def _():
+            copy_to(entering.at[h], entering.at[h], e_send.at[h], e_recv.at[h],
+                    {"seq": base + swapped(h)}).wait_recv()
+        rows_here = dot(qe[h], entering[h]) + own[h]
         for t in range(4):
-            att[t, h] = mine[t * C : (t + 1) * C].astype(BF16)
+            att[t, h] = rows_here[t * C : (t + 1) * C].astype(BF16)
         for j in (2, 1, 3):
             out_copy(h, j).start()
 
     lax.fori_loop(0, 2, lambda two, _: compute(two), 0)
     loads[4].wait()
     qs[...] = q_ref[...].astype(F32).reshape(2048, C)
-    late = member // 2
+
+    def step_out(h, _):
+        apply(h)
+        return 0
 
     def step(t, _):
         compute_rows(t)
+
+        @pl.when(t == 3)
+        def _():
+            lax.fori_loop(0, 2, step_out, 0)
 
         @pl.when((t == 0) & (late == 1))
         def _():
@@ -396,11 +410,7 @@
 
     lax.fori_loop(0, 4, step, 0)
 
-    def step_out(h, _):
-        apply(h)
-        return 0
-
-    lax.fori_loop(0, 4, step_out, 0)
+    lax.fori_loop(2, 4, step_out, 0)
 
     ra2(across).wait_recv()
     over(across, 0, 4).start()
@@ -413,7 +423,7 @@
     ra2(left).wait_send()
     lb2(right).wait_send()
     for j in (1, 2, 3):
-        item_copy(member ^ j).wait_send()
+        item_copy(swapped(member ^ j)).wait_send()
         pair_copy(j).wait_send()
         enter_copy(j).wait_send()
 

time: 55.5 us -> 53.6 us (0.966)
  the two profiles are of different devices: /device:TPU:70 before, /device:TPU:1 now
where the time goes in v6:
time: 53.6 us; the launch traced here: 53.5 us
  Pallas kernels  52.7 us (98%)
  local copies, waits for them, and re-layouts  0.8 us (1%)
    pallas_call x1, Pallas kernels, layer(): pl.pallas_call(layer_kernel, out_shape=jax.ShapeDtypeStruct((128, 2048),...  52.7 us

profile of v6, /device:TPU:1, one launch (start us, length us, event | category | flops | bytes accessed | tf_op | source)
XLA Modules:
  0.0 53.5 jit_solution(7504974847964198924)
XLA Ops:
  0.0 52.7 %shard_map.64 = bf16[128,2048]{1,0:T(8,128)(2,1)S(1)} custom-call(bf16[512,4,128]{2,1,0:T(4,128)(2,1)} %q_in.1, bf16[512,4,128]{2,1,0:T(4,128)(2,1)} %k_in.1, bf16[512,4,128]{2,1,0:T(4,128)(2,1)} %v_in.1, f32[4,512]{1,0:T(4,128)} %b_in.1, f32[4,512]{1,0:T(4,128)} %d_in.1, bf16[4,128,2048]{2,1,0:T(8,128)(2,1)} %bitcast.1), custom_call_target="tpu_custom_call" | custom-call | tf_op jit(solution)/shard_map/pallas_call | solution.py:463
  52.7 0.8 %copy.8 = bf16[128,2048]{1,0:T(8,128)(2,1)} copy(bf16[128,2048]{1,0:T(8,128)(2,1)S(1)} %shard_map.64) | data formatting | bytes 1048576

commit v7 on v6

--- a/solution.py
+++ b/solution.py
@@ -222,8 +222,6 @@
         pl.semaphore_wait(barrier, len(friends))
         ra(head).start()
         lb(head).start()
-        rb(head).start()
-        la(head).start()
 
     def item_copy(h):
         return copy_to(items.at[h], group.at[member], g_send.at[h], g_recv.at[member], {"seq": base + swapped(h)})
@@ -266,6 +264,11 @@
             @pl.when(two == 0)
             def _():
                 greet()
+
+            @pl.when(two == 1)
+            def _():
+                rb(head).start()
+                la(head).start()
 
             @pl.when((two == 1) & (late == 0))
             def _():
@@ -364,6 +367,12 @@
             out_copy(h, j).start()
 
     lax.fori_loop(0, 2, lambda two, _: compute(two), 0)
+    ra(left).wait_recv()
+    ra2(left).start()
+    lb(right).wait_recv()
+    lb2(right).start()
+    over(left, 0, 0).start()
+    over(right, 1, 1).start()
     loads[4].wait()
     qs[...] = q_ref[...].astype(F32).reshape(2048, C)
 
@@ -391,31 +400,25 @@
             scan_lines()
 
         @pl.when(t == 1)
-        def _():
-            ra(left).wait_recv()
-            ra2(left).start()
-            lb(right).wait_recv()
-            lb2(right).start()
-            over(left, 0, 0).start()
-            over(right, 1, 1).start()
-
-        @pl.when(t == 2)
         def _():
             rb(left).wait_recv()
             over(left, 1, 2).start()
             la(right).wait_recv()
             over(right, 0, 3).start()
 
+        @pl.when(t == 2)
+        def _():
+            ra2(across).wait_recv()
+            over(across, 0, 4).start()
+            lb2(across).wait_recv()
+            over(across, 1, 5).start()
+
         return 0
 
     lax.fori_loop(0, 4, step, 0)
 
     lax.fori_loop(2, 4, step_out, 0)
 
-    ra2(across).wait_recv()
-    over(across, 0, 4).start()
-    lb2(across).wait_recv()
-    over(across, 1, 5).start()
     ra(head).wait_send()
     lb(head).wait_send()
     rb(head).wait_send()

time: 53.6 us -> 54.4 us (1.015)
  the two profiles are of different devices: /device:TPU:1 before, /device:TPU:6 now
where the time goes in v7:
time: 54.4 us; the launch traced here: 54.3 us
  Pallas kernels  53.5 us (98%)
  local copies, waits for them, and re-layouts  0.8 us (1%)
    pallas_call x1, Pallas kernels, layer(): pl.pallas_call(layer_kernel, out_shape=jax.ShapeDtypeStruct((128, 2048),...  53.5 us

profile of v7, /device:TPU:6, one launch (start us, length us, event | category | flops | bytes accessed | tf_op | source)
XLA Modules:
  0.0 54.3 jit_solution(8692611775934426074)
XLA Ops:
  0.0 53.5 %shard_map.64 = bf16[128,2048]{1,0:T(8,128)(2,1)S(1)} custom-call(bf16[512,4,128]{2,1,0:T(4,128)(2,1)} %q_in.1, bf16[512,4,128]{2,1,0:T(4,128)(2,1)} %k_in.1, bf16[512,4,128]{2,1,0:T(4,128)(2,1)} %v_in.1, f32[4,512]{1,0:T(4,128)} %b_in.1, f32[4,512]{1,0:T(4,128)} %d_in.1, bf16[4,128,2048]{2,1,0:T(8,128)(2,1)} %bitcast.1), custom_call_target="tpu_custom_call" | custom-call | tf_op jit(solution)/shard_map/pallas_call | solution.py:466
  53.5 0.8 %copy.8 = bf16[128,2048]{1,0:T(8,128)(2,1)} copy(bf16[128,2048]{1,0:T(8,128)(2,1)S(1)} %shard_map.64) | data formatting | bytes 1048576

commit v8 on v6

--- a/solution.py
+++ b/solution.py
@@ -7,7 +7,6 @@
 
 C = 128
 LEVELS = (2, 4, 8, 16, 32, 64)
-MIDDLE = 2
 F32, BF16 = jnp.float32, jnp.bfloat16
 
 
@@ -75,8 +74,7 @@
         yh = [halves(y) for y in ys]
         zs = [exact_square(x, y) for x, y in zip(xh, yh)]
         xs = [x - z for x, z in zip(xs, zs)]
-        if i == MIDDLE:
-            middle()
+        middle(i)
     return xs
 
 
@@ -202,28 +200,52 @@
     def copy_to(source, target, send_sem, recv_sem, to):
         return pltpu.make_async_remote_copy(source, target, send_sem, recv_sem, device_id=to, device_id_type=MESH)
 
-    def quarter(of, part):
-        return weight.at[of, 2 * core + part]
-
     sibling = {"seq": seq ^ 1}
     to_right, to_left = {"head": right}, {"head": left}
-    ra = lambda of: copy_to(quarter(of, 0), quarter(of, 0), w_send.at[0], w_recv.at[0], to_right)
-    lb = lambda of: copy_to(quarter(of, 1), quarter(of, 1), w_send.at[1], w_recv.at[1], to_left)
-    rb = lambda of: copy_to(quarter(of, 1), quarter(of, 1), w_send.at[2], w_recv.at[2], to_right)
-    la = lambda of: copy_to(quarter(of, 0), quarter(of, 0), w_send.at[3], w_recv.at[3], to_left)
-    ra2 = lambda of: copy_to(quarter(of, 0), quarter(of, 0), w_send.at[4], w_recv.at[4], to_right)
-    lb2 = lambda of: copy_to(quarter(of, 1), quarter(of, 1), w_send.at[5], w_recv.at[5], to_left)
-
-    def over(of, part, i):
-        return copy_to(quarter(of, part), quarter(of, part), w_send.at[6 + i], w_recv.at[6 + i], sibling)
+    to_next, to_last = {"seq": (seq + 16) % 64}, {"seq": (seq + 48) % 64}
+    block = 2 * core + line % 2
+    block_x = 2 * core + 1 - line % 2
+    top, low = pl.ds(0, 64), pl.ds(64, 64)
+
+    def same(ref, i, to):
+        return copy_to(ref, ref, w_send.at[i], w_recv.at[i], to)
+
+    def go_right(of):
+        return same(weight.at[of, block], 0, to_right)
+
+    def go_left(of):
+        return same(weight.at[of, block], 1, to_left)
+
+    def relay_right(of):
+        return same(weight.at[of, block, top], 2, to_right)
+
+    def relay_left(of):
+        return same(weight.at[of, block, low], 3, to_left)
+
+    def go_next(of, i, at_block=block):
+        return same(weight.at[of, at_block, top], 4 + i, to_next)
+
+    def go_last(of, i, at_block=block):
+        return same(weight.at[of, at_block, low], 7 + i, to_last)
+
+    def over(of, i, at_block):
+        return same(weight.at[of, at_block], 10 + i, sibling)
+
+    def share(of, i):
+        go_next(of, i).start()
+        go_last(of, i).start()
+        over(of, i, block).start()
+
+    def share_x(of, i):
+        go_next(of, i, block_x).wait_recv()
+        go_last(of, i, block_x).wait_recv()
+        over(of, 3 + i, block_x).start()
 
     def greet():
         load.wait()
         pl.semaphore_wait(barrier, len(friends))
-        ra(head).start()
-        lb(head).start()
-        rb(head).start()
-        la(head).start()
+        go_right(head).start()
+        go_left(head).start()
 
     def item_copy(h):
         return copy_to(items.at[h], group.at[member], g_send.at[h], g_recv.at[member], {"seq": base + swapped(h)})
@@ -262,14 +284,16 @@
 
             return at(ks, h), at(vs, h), four(b_ref), four(d_ref), keep
 
-        def middle():
-            @pl.when(two == 0)
-            def _():
-                greet()
-
-            @pl.when((two == 1) & (late == 0))
-            def _():
-                scan_group()
+        def middle(i):
+            if i == 0:
+                @pl.when(two == 0)
+                def _():
+                    greet()
+
+            if i == 3:
+                @pl.when((two == 1) & (late == 0))
+                def _():
+                    scan_group()
 
         heads = [2 * two, 2 * two + 1]
         for h, result in zip(heads, key_side([head_of(h) for h in heads], masks, middle)):
@@ -364,6 +388,12 @@
             out_copy(h, j).start()
 
     lax.fori_loop(0, 2, lambda two, _: compute(two), 0)
+    go_right(left).wait_recv()
+    relay_right(left).start()
+    go_left(right).wait_recv()
+    relay_left(right).start()
+    share(left, 0)
+    share(right, 1)
     loads[4].wait()
     qs[...] = q_ref[...].astype(F32).reshape(2048, C)
 
@@ -392,19 +422,14 @@
 
         @pl.when(t == 1)
         def _():
-            ra(left).wait_recv()
-            ra2(left).start()
-            lb(right).wait_recv()
-            lb2(right).start()
-            over(left, 0, 0).start()
-            over(right, 1, 1).start()
+            relay_right(across).wait_recv()
+            relay_left(across).wait_recv()
+            share(across, 2)
 
         @pl.when(t == 2)
         def _():
-            rb(left).wait_recv()
-            over(left, 1, 2).start()
-            la(right).wait_recv()
-            over(right, 0, 3).start()
+            share_x(left, 0)
+            share_x(right, 1)
 
         return 0
 
@@ -412,16 +437,11 @@
 
     lax.fori_loop(2, 4, step_out, 0)
 
-    ra2(across).wait_recv()
-    over(across, 0, 4).start()
-    lb2(across).wait_recv()
-    over(across, 1, 5).start()
-    ra(head).wait_send()
-    lb(head).wait_send()
-    rb(head).wait_send()
-    la(head).wait_send()
-    ra2(left).wait_send()
-    lb2(right).wait_send()
+    share_x(across, 2)
+    go_right(head).wait_send()
+    go_left(head).wait_send()
+    relay_right(left).wait_send()
+    relay_left(right).wait_send()
     for j in (1, 2, 3):
         item_copy(swapped(member ^ j)).wait_send()
         pair_copy(j).wait_send()
@@ -431,12 +451,12 @@
         def _():
             line_copy(j).wait_send()
 
-    def other_half(of, part):
-        return weight.at[of, 2 * (1 - core) + part]
-
-    for i, (of, part) in enumerate(((left, 0), (right, 1), (left, 1), (right, 0), (across, 0), (across, 1))):
-        over(of, part, i).wait_send()
-        copy_to(other_half(of, part), other_half(of, part), w_send.at[6 + i], w_recv.at[6 + i], sibling).wait_recv()
+    for i, of in enumerate((left, right, across)):
+        go_next(of, i).wait_send()
+        go_last(of, i).wait_send()
+        for k, at_block in ((0, block), (3, block_x)):
+            over(of, i + k, at_block).wait_send()
+            over(of, i + k, (at_block + 2) % 4).wait_recv()
 
     def product(heads, cols):
         rows_in = jnp.concatenate(
@@ -490,7 +510,7 @@
             pltpu.VMEM((4 * C, 2 * C), BF16),
             pltpu.VMEM((4 * C, C), F32),
             pltpu.VMEM((C, C), F32),
-            dma((5,)), dma, dma((12,)), dma((12,)),
+            dma((5,)), dma, dma((16,)), dma((16,)),
         ] + [dma((4,))] * 8 + [dma((4, 4))] * 2,
         compiler_params=pltpu.CompilerParams(
             collective_id=0, has_side_effects=True, vmem_limit_bytes=40 * 2**20),

time: 53.6 us -> 52.5 us (0.979)
  the two profiles are of different devices: /device:TPU:1 before, /device:TPU:6 now
where the time goes in v8:
time: 52.5 us; the launch traced here: 51.7 us
  Pallas kernels  50.9 us (97%)
  local copies, waits for them, and re-layouts  0.8 us (2%)
    pallas_call x1, Pallas kernels, layer(): pl.pallas_call(layer_kernel, out_shape=jax.ShapeDtypeStruct((128, 2048),...  50.9 us

profile of v8, /device:TPU:6, one launch (start us, length us, event | category | flops | bytes accessed | tf_op | source)
XLA Modules:
  0.0 51.7 jit_solution(14407597627629455554)
XLA Ops:
  0.0 50.9 %shard_map.64 = bf16[128,2048]{1,0:T(8,128)(2,1)S(1)} custom-call(bf16[512,4,128]{2,1,0:T(4,128)(2,1)} %q_in.1, bf16[512,4,128]{2,1,0:T(4,128)(2,1)} %k_in.1, bf16[512,4,128]{2,1,0:T(4,128)(2,1)} %v_in.1, f32[4,512]{1,0:T(4,128)} %b_in.1, f32[4,512]{1,0:T(4,128)} %d_in.1, bf16[4,128,2048]{2,1,0:T(8,128)(2,1)} %bitcast.1), custom_call_target="tpu_custom_call" | custom-call | tf_op jit(solution)/shard_map/pallas_call | solution.py:483
  50.9 0.8 %copy.8 = bf16[128,2048]{1,0:T(8,128)(2,1)} copy(bf16[128,2048]{1,0:T(8,128)(2,1)S(1)} %shard_map.64) | data formatting | bytes 1048576

commit v9 on v8

--- a/solution.py
+++ b/solution.py
@@ -194,8 +194,6 @@
     fill_masks(masks)
     for copy in loads[:4]:
         copy.wait()
-    for source, target in ((k_ref, ks), (v_ref, vs)):
-        target[...] = source[...].astype(F32).reshape(2048, C)
 
     def copy_to(source, target, send_sem, recv_sem, to):
         return pltpu.make_async_remote_copy(source, target, send_sem, recv_sem, device_id=to, device_id_type=MESH)
@@ -241,11 +239,12 @@
         go_last(of, i, block_x).wait_recv()
         over(of, 3 + i, block_x).start()
 
-    def greet():
-        load.wait()
-        pl.semaphore_wait(barrier, len(friends))
-        go_right(head).start()
-        go_left(head).start()
+    load.wait()
+    pl.semaphore_wait(barrier, len(friends))
+    go_right(head).start()
+    go_left(head).start()
+    for source, target in ((k_ref, ks), (v_ref, vs)):
+        target[...] = source[...].astype(F32).reshape(2048, C)
 
     def item_copy(h):
         return copy_to(items.at[h], group.at[member], g_send.at[h], g_recv.at[member], {"seq": base + swapped(h)})
@@ -285,15 +284,20 @@
             return at(ks, h), at(vs, h), four(b_ref), four(d_ref), keep
 
         def middle(i):
-            if i == 0:
-                @pl.when(two == 0)
-                def _():
-                    greet()
-
             if i == 3:
                 @pl.when((two == 1) & (late == 0))
                 def _():
                     scan_group()
+
+            if i == 4:
+                @pl.when(two == 1)
+                def _():
+                    go_right(left).wait_recv()
+                    relay_right(left).start()
+                    go_left(right).wait_recv()
+                    relay_left(right).start()
+                    share(left, 0)
+                    share(right, 1)
 
         heads = [2 * two, 2 * two + 1]
         for h, result in zip(heads, key_side([head_of(h) for h in heads], masks, middle)):
@@ -388,12 +392,6 @@
             out_copy(h, j).start()
 
     lax.fori_loop(0, 2, lambda two, _: compute(two), 0)
-    go_right(left).wait_recv()
-    relay_right(left).start()
-    go_left(right).wait_recv()
-    relay_left(right).start()
-    share(left, 0)
-    share(right, 1)
     loads[4].wait()
     qs[...] = q_ref[...].astype(F32).reshape(2048, C)
 
@@ -420,24 +418,27 @@
         def _():
             scan_lines()
 
-        @pl.when(t == 1)
+        @pl.when(t == 0)
         def _():
             relay_right(across).wait_recv()
             relay_left(across).wait_recv()
             share(across, 2)
 
-        @pl.when(t == 2)
+        @pl.when(t == 1)
         def _():
             share_x(left, 0)
             share_x(right, 1)
 
+        @pl.when(t == 2)
+        def _():
+            share_x(across, 2)
+
         return 0
 
     lax.fori_loop(0, 4, step, 0)
 
     lax.fori_loop(2, 4, step_out, 0)
 
-    share_x(across, 2)
     go_right(head).wait_send()
     go_left(head).wait_send()
     relay_right(left).wait_send()

time: 52.5 us -> 56.4 us (1.074)
  Pallas kernels: 50.9 us -> 55.3 us
    pallas_call x1, Pallas kernels: 50.9 us -> 55.3 us  [layer(): pl.pallas_call(layer_kernel, out_shape=jax.ShapeDtypeStruct((128, 2048),...]
where the time goes in v9:
time: 56.4 us; the launch traced here: 56.1 us
  Pallas kernels  55.3 us (98%)
  local copies, waits for them, and re-layouts  0.8 us (1%)
    pallas_call x1, Pallas kernels, layer(): pl.pallas_call(layer_kernel, out_shape=jax.ShapeDtypeStruct((128, 2048),...  55.3 us

profile of v9, /device:TPU:6, one launch (start us, length us, event | category | flops | bytes accessed | tf_op | source)
XLA Modules:
  0.0 56.1 jit_solution(8963867423079924229)
XLA Ops:
  0.0 55.3 %shard_map.64 = bf16[128,2048]{1,0:T(8,128)(2,1)S(1)} custom-call(bf16[512,4,128]{2,1,0:T(4,128)(2,1)} %q_in.1, bf16[512,4,128]{2,1,0:T(4,128)(2,1)} %k_in.1, bf16[512,4,128]{2,1,0:T(4,128)(2,1)} %v_in.1, f32[4,512]{1,0:T(4,128)} %b_in.1, f32[4,512]{1,0:T(4,128)} %d_in.1, bf16[4,128,2048]{2,1,0:T(8,128)(2,1)} %bitcast.1), custom_call_target="tpu_custom_call" | custom-call | tf_op jit(solution)/shard_map/pallas_call | solution.py:484
  55.4 0.8 %copy.8 = bf16[128,2048]{1,0:T(8,128)(2,1)} copy(bf16[128,2048]{1,0:T(8,128)(2,1)S(1)} %shard_map.64) | data formatting | bytes 1048576

commit v10 on v8

--- a/solution.py
+++ b/solution.py
@@ -194,8 +194,6 @@
     fill_masks(masks)
     for copy in loads[:4]:
         copy.wait()
-    for source, target in ((k_ref, ks), (v_ref, vs)):
-        target[...] = source[...].astype(F32).reshape(2048, C)
 
     def copy_to(source, target, send_sem, recv_sem, to):
         return pltpu.make_async_remote_copy(source, target, send_sem, recv_sem, device_id=to, device_id_type=MESH)
@@ -241,11 +239,12 @@
         go_last(of, i, block_x).wait_recv()
         over(of, 3 + i, block_x).start()
 
-    def greet():
-        load.wait()
-        pl.semaphore_wait(barrier, len(friends))
-        go_right(head).start()
-        go_left(head).start()
+    load.wait()
+    pl.semaphore_wait(barrier, len(friends))
+    go_right(head).start()
+    go_left(head).start()
+    for source, target in ((k_ref, ks), (v_ref, vs)):
+        target[...] = source[...].astype(F32).reshape(2048, C)
 
     def item_copy(h):
         return copy_to(items.at[h], group.at[member], g_send.at[h], g_recv.at[member], {"seq": base + swapped(h)})
@@ -285,11 +284,6 @@
             return at(ks, h), at(vs, h), four(b_ref), four(d_ref), keep
 
         def middle(i):
-            if i == 0:
-                @pl.when(two == 0)
-                def _():
-                    greet()
-
             if i == 3:
                 @pl.when((two == 1) & (late == 0))
                 def _():

time: 52.5 us -> 52.8 us (level)
  no operation moved by 1% of the time
where the time goes in v10:
time: 52.8 us; the launch traced here: 51.9 us
  Pallas kernels  51.1 us (97%)
  local copies, waits for them, and re-layouts  0.8 us (2%)
    pallas_call x1, Pallas kernels, layer(): pl.pallas_call(layer_kernel, out_shape=jax.ShapeDtypeStruct((128, 2048),...  51.1 us

profile of v10, /device:TPU:6, one launch (start us, length us, event | category | flops | bytes accessed | tf_op | source)
XLA Modules:
  0.0 51.9 jit_solution(181285499550362358)
XLA Ops:
  0.0 51.1 %shard_map.64 = bf16[128,2048]{1,0:T(8,128)(2,1)S(1)} custom-call(bf16[512,4,128]{2,1,0:T(4,128)(2,1)} %q_in.1, bf16[512,4,128]{2,1,0:T(4,128)(2,1)} %k_in.1, bf16[512,4,128]{2,1,0:T(4,128)(2,1)} %v_in.1, f32[4,512]{1,0:T(4,128)} %b_in.1, f32[4,512]{1,0:T(4,128)} %d_in.1, bf16[4,128,2048]{2,1,0:T(8,128)(2,1)} %bitcast.1), custom_call_target="tpu_custom_call" | custom-call | tf_op jit(solution)/shard_map/pallas_call | solution.py:477
  51.1 0.8 %copy.8 = bf16[128,2048]{1,0:T(8,128)(2,1)} copy(bf16[128,2048]{1,0:T(8,128)(2,1)S(1)} %shard_map.64) | data formatting | bytes 1048576

commit v11 on v8

--- a/solution.py
+++ b/solution.py
@@ -431,13 +431,16 @@
             share_x(left, 0)
             share_x(right, 1)
 
+        @pl.when(t == 3)
+        def _():
+            share_x(across, 2)
+
         return 0
 
     lax.fori_loop(0, 4, step, 0)
 
     lax.fori_loop(2, 4, step_out, 0)
 
-    share_x(across, 2)
     go_right(head).wait_send()
     go_left(head).wait_send()
     relay_right(left).wait_send()

time: 52.5 us -> 52.5 us (level)
  no operation moved by 1% of the time
where the time goes in v11:
time: 52.5 us; the launch traced here: 51.7 us
  Pallas kernels  50.9 us (97%)
  local copies, waits for them, and re-layouts  0.8 us (2%)
    pallas_call x1, Pallas kernels, layer(): pl.pallas_call(layer_kernel, out_shape=jax.ShapeDtypeStruct((128, 2048),...  50.9 us

profile of v11, /device:TPU:6, one launch (start us, length us, event | category | flops | bytes accessed | tf_op | source)
XLA Modules:
  0.0 51.7 jit_solution(5070684003737631501)
XLA Ops:
  0.0 50.9 %shard_map.64 = bf16[128,2048]{1,0:T(8,128)(2,1)S(1)} custom-call(bf16[512,4,128]{2,1,0:T(4,128)(2,1)} %q_in.1, bf16[512,4,128]{2,1,0:T(4,128)(2,1)} %k_in.1, bf16[512,4,128]{2,1,0:T(4,128)(2,1)} %v_in.1, f32[4,512]{1,0:T(4,128)} %b_in.1, f32[4,512]{1,0:T(4,128)} %d_in.1, bf16[4,128,2048]{2,1,0:T(8,128)(2,1)} %bitcast.1), custom_call_target="tpu_custom_call" | custom-call | tf_op jit(solution)/shard_map/pallas_call | solution.py:486
  50.9 0.8 %copy.8 = bf16[128,2048]{1,0:T(8,128)(2,1)} copy(bf16[128,2048]{1,0:T(8,128)(2,1)S(1)} %shard_map.64) | data formatting | bytes 1048576

commit v12 on v8

--- a/solution.py
+++ b/solution.py
@@ -451,30 +451,36 @@
         def _():
             line_copy(j).wait_send()
 
-    for i, of in enumerate((left, right, across)):
+    def settle(of, i):
         go_next(of, i).wait_send()
         go_last(of, i).wait_send()
         for k, at_block in ((0, block), (3, block_x)):
             over(of, i + k, at_block).wait_send()
             over(of, i + k, (at_block + 2) % 4).wait_recv()
 
-    def product(heads, cols):
+    def product(heads, steps, cols):
         rows_in = jnp.concatenate(
-            [att[head, h] if j == 0 else arrived[j, h] for j in range(4) for h in heads], axis=1)
+            [att[head, h] if j == 0 else arrived[j, h] for j in steps for h in heads], axis=1)
         rows_w = jnp.concatenate(
-            [weight[(head + 4 - j) % 4, h, :, cols] for j in range(4) for h in heads], axis=0)
+            [weight[(head + 4 - j) % 4, h, :, cols] for j in steps for h in heads], axis=0)
         return dot(rows_in, rows_w)
 
+    settle(left, 0)
+    settle(right, 1)
     for h in range(3):
         for j in (1, 3, 2):
             out_copy(h, j).wait()
     for n in range(4):
-        total[:, n * 512 : (n + 1) * 512] = product((0, 1, 2), slice(n * 512, (n + 1) * 512))
+        total[:, n * 512 : (n + 1) * 512] = product((0, 1, 2), (0, 1, 3), slice(n * 512, (n + 1) * 512))
     for j in (1, 3, 2):
         out_copy(3, j).wait()
     for n in range(4):
         cols = slice(n * 512, (n + 1) * 512)
-        out_ref[:, cols] = (total[:, cols] + product((3,), cols)).astype(BF16)
+        total[:, cols] = total[:, cols] + product((3,), (0, 1, 3), cols)
+    settle(across, 2)
+    for n in range(4):
+        cols = slice(n * 512, (n + 1) * 512)
+        out_ref[:, cols] = (total[:, cols] + product((0, 1, 2, 3), (2,), cols)).astype(BF16)
 
 
 def layer(q, k, v, b, d, w):

time: 52.5 us -> 52.8 us (level)
  no operation moved by 1% of the time
where the time goes in v12:
time: 52.8 us; the launch traced here: 52 us
  Pallas kernels  51.2 us (97%)
  local copies, waits for them, and re-layouts  0.8 us (2%)
    pallas_call x1, Pallas kernels, layer(): pl.pallas_call(layer_kernel, out_shape=jax.ShapeDtypeStruct((128, 2048),...  51.2 us

profile of v12, /device:TPU:6, one launch (start us, length us, event | category | flops | bytes accessed | tf_op | source)
XLA Modules:
  0.0 52.0 jit_solution(821532162589677275)
XLA Ops:
  0.0 51.2 %shard_map.64 = bf16[128,2048]{1,0:T(8,128)(2,1)S(1)} custom-call(bf16[512,4,128]{2,1,0:T(4,128)(2,1)} %q_in.1, bf16[512,4,128]{2,1,0:T(4,128)(2,1)} %k_in.1, bf16[512,4,128]{2,1,0:T(4,128)(2,1)} %v_in.1, f32[4,512]{1,0:T(4,128)} %b_in.1, f32[4,512]{1,0:T(4,128)} %d_in.1, bf16[4,128,2048]{2,1,0:T(8,128)(2,1)} %bitcast.1), custom_call_target="tpu_custom_call" | custom-call | tf_op jit(solution)/shard_map/pallas_call | solution.py:489
  51.2 0.8 %copy.8 = bf16[128,2048]{1,0:T(8,128)(2,1)} copy(bf16[128,2048]{1,0:T(8,128)(2,1)S(1)} %shard_map.64) | data formatting | bytes 1048576
